TPU v7x, 128 devices: a whole 4x4x4 slice. The times are simulated.
128 devices in a mesh: rec: 4 (over y), tm: 32 (over x, z, core).
Axes of the slice: x: 4, y: 4, z: 4, core: 2. Of those that a mesh axis runs over, the one named last changes fastest.
Arguments:
- token_values: bfloat16 [4, 8192, 2048], P('rec', 'tm'), may hold values from -6 to 6
- write_keys: bfloat16 [4, 8192, 128], P('rec', 'tm'), may hold values from -0.125 to 0.125
- read_queries: bfloat16 [4, 8192, 128], P('rec', 'tm'), may hold values from -6 to 6
- step_sizes: float32 [4, 32, 8192], P('rec', None, 'tm'), may hold values from 0.25 to 3
- decay_log: float32 [32], replicated
- skip_gain: float32 [32], replicated, may hold values from 0.5 to 2
- out_weight: bfloat16 [2048, 1024], replicated, may hold values from -0.125 to 0.125
- out_grad: bfloat16 [4, 8192, 1024], P('rec', 'tm'), may hold values from -6 to 6
Outputs:
- grad_values: float32 [4, 8192, 2048], P('rec', 'tm')
- grad_keys: float32 [4, 8192, 128], P('rec', 'tm')
- grad_queries: float32 [4, 8192, 128], P('rec', 'tm')
- grad_steps: float32 [4, 32, 8192], P('rec', None, 'tm')
- grad_decay: float32 [32], replicated
- grad_skip: float32 [32], replicated
- grad_weight: float32 [2048, 1024], P('tm')
All inputs are finite; a program needn't handle non-finite values.
Results may differ from a plain program's by a relative error of at most 0.0029.
Values sent between devices are 32-bit elements; how exact they have to be, the bound alone decides.
A program may use at most 256 MiB of HBM per device.

v0:
```python
from functools import partial

import jax
import jax.numpy as jnp
from jax import lax
from jax.sharding import PartitionSpec as P

SPAN = 256


def prefix(value, axis, join, neutral, backward):
    count, mine = (lax.axis_size(axis), lax.axis_index(axis))
    pieces = jax.tree.map(lambda part: lax.all_gather(part, axis), value)
    if backward:
        pieces = jax.tree.map(lambda part: part[::-1], pieces)
        mine = count - 1 - mine
    so_far = jax.tree.map(
        lambda part, zero: jnp.full_like(part, 0) + jnp.asarray(zero, part.dtype), value, neutral
    )

    def hop(position, so_far):
        longer = join(so_far, jax.tree.map(lambda part: part[position], pieces))
        return jax.tree.map(lambda new, old: jnp.where(position < mine, new, old), longer, so_far)

    return lax.fori_loop(0, count - 1, hop, so_far)


def block_terms(element):
    scaled, key_rows, queries, running = element
    row_iota = lax.broadcasted_iota(jnp.int32, (SPAN, SPAN), 0)
    col_iota = lax.broadcasted_iota(jnp.int32, (SPAN, SPAN), 1)
    causal = row_iota >= col_iota
    log_gap = running[:, :, None] - running[:, None, :]
    decay_mat = jnp.where(causal, jnp.exp(jnp.where(causal, log_gap, 0.0)), 0.0)
    scores = jnp.dot(queries, key_rows.T, precision=lax.Precision.HIGHEST)
    inside_offset = jnp.einsum(
        "hij,jhp->ihp", decay_mat * scores[None], scaled, precision=lax.Precision.HIGHEST
    )
    to_end = jnp.exp(running[:, -1:] - running)
    weighted = scaled * to_end.T[:, :, None]
    block_state = jnp.einsum("jhp,jn->hpn", weighted, key_rows, precision=lax.Precision.HIGHEST)
    return (inside_offset, block_state)


def segment_forward(values, key_rows, queries, step_rows, decay_vec, skip_vec, state_in):
    head_count, length = step_rows.shape
    head_width = values.shape[1] // head_count
    state_width = key_rows.shape[1]
    blocks = length // SPAN
    step_rate = -jnp.exp(decay_vec)[:, None] * step_rows
    running = jnp.cumsum(step_rate.reshape(head_count, blocks, SPAN), axis=2).transpose(1, 0, 2)
    scaled = values.reshape(length, head_count, head_width) * step_rows.T[:, :, None]
    scaled = scaled.reshape(blocks, SPAN, head_count, head_width)
    key_blocks = key_rows.reshape(blocks, SPAN, state_width)
    query_blocks = queries.reshape(blocks, SPAN, state_width)
    inside_offset, block_states = lax.map(block_terms, (scaled, key_blocks, query_blocks, running))
    totals = jnp.exp(running[:, :, -1])

    def advance(carried, element):
        total, block_state = element
        return (total[:, None, None] * carried + block_state, carried)

    end_state, before = lax.scan(advance, state_in, (totals, block_states))
    across = jnp.einsum("kin,khpn->kihp", query_blocks, before, precision=lax.Precision.HIGHEST)
    across = across * jnp.exp(running).transpose(0, 2, 1)[:, :, :, None]
    mixed_out = (inside_offset + across).reshape(length, head_count * head_width)
    mixed_out = mixed_out + jnp.repeat(skip_vec, head_width)[None, :] * values
    return (mixed_out, end_state)


def chain(earlier, later):
    early_decay, early_state = earlier
    late_decay, late_state = later
    return (early_decay * late_decay, late_decay[:, :, None, None] * early_state + late_state)


def local(
    token_values, write_keys, read_queries, step_sizes, decay_log, skip_gain, out_weight, out_grad
):
    rec_count, head_count, length = step_sizes.shape
    inner = token_values.shape[2]
    head_width = inner // head_count
    step_rate = -jnp.exp(decay_log)[None, :, None] * step_sizes
    running = jnp.cumsum(step_rate, axis=2)
    device_decay = jnp.exp(running[:, :, -1])
    to_end = jnp.exp(running[:, :, -1:] - running) * step_sizes
    weighted = token_values.astype(jnp.float32).reshape(rec_count, length, head_count, head_width)
    weighted = weighted * to_end.transpose(0, 2, 1)[:, :, :, None]
    local_state = jnp.einsum(
        "rshp,rsn->rhpn", weighted, write_keys.astype(jnp.float32), precision=lax.Precision.HIGHEST
    )
    identity = (jnp.ones_like(device_decay), jnp.zeros_like(local_state))
    state_in = prefix((device_decay, local_state), "tm", chain, identity, False)[1]
    forward = partial(segment_forward, state_in=state_in[0])
    (mixer_out, end_state), pullback = jax.vjp(
        forward,
        token_values[0].astype(jnp.float32),
        write_keys[0].astype(jnp.float32),
        read_queries[0].astype(jnp.float32),
        step_sizes[0],
        decay_log,
        skip_gain,
    )
    grad_mixer = jnp.dot(out_grad[0], out_weight.T, preferred_element_type=jnp.float32)
    entry_grad = jnp.einsum(
        "sn,shp,hs->hpn",
        read_queries[0].astype(jnp.float32),
        grad_mixer.reshape(length, head_count, head_width),
        jnp.exp(running[0]),
        precision=lax.Precision.HIGHEST,
    )
    stored_rows = mixer_out.astype(jnp.bfloat16)
    entry_grads = [entry_grad]
    after = prefix((device_decay, jnp.stack(entry_grads)), "tm", chain, identity, True)[1]
    grads = [pullback((grad_mixer, after[0]))]
    grad_values = jnp.stack([entry[0] for entry in grads])
    grad_keys = jnp.stack([entry[1] for entry in grads])
    grad_queries = jnp.stack([entry[2] for entry in grads])
    grad_steps = jnp.stack([entry[3] for entry in grads])
    decay_part = jnp.sum(jnp.stack([entry[4] for entry in grads]), axis=0)
    skip_part = jnp.sum(jnp.stack([entry[5] for entry in grads]), axis=0)
    grad_decay, grad_skip = lax.psum((decay_part, skip_part), ("rec", "tm"))
    upstream = out_grad.reshape(rec_count * length, out_grad.shape[2])
    tm_part = lax.psum_scatter(
        jnp.dot(stored_rows.T, upstream, preferred_element_type=jnp.float32),
        "tm",
        scatter_dimension=0,
        tiled=True,
    )
    grad_weight = lax.psum(tm_part, "rec")
    return (grad_values, grad_keys, grad_queries, grad_steps, grad_decay, grad_skip, grad_weight)


def solution(mesh):
    placed = (
        P("rec", "tm", None),
        P("rec", "tm", None),
        P("rec", "tm", None),
        P("rec", None, "tm"),
        P(),
        P(),
        P(),
        P("rec", "tm", None),
    )
    return jax.shard_map(
        local,
        mesh=mesh,
        in_specs=placed,
        out_specs=(
            P("rec", "tm", None),
            P("rec", "tm", None),
            P("rec", "tm", None),
            P("rec", None, "tm"),
            P(),
            P(),
            P("tm", None),
        ),
        check_vma=False,
    )
```

profile of v0, /device:TPU:0, one launch (start us, length us, event | category | flops | bytes accessed | tf_op | source)
XLA Modules:
  0.0 500.0 jit_solution(7903015108852960374)
XLA Ops:
  9.7 4.8 fusion.50
  14.5 2.0 copy.196
  16.5 2.2 fusion.25
  20.3 1.9 copy.209
  22.5 1.9 copy.219
  25.8 3.0 copy.208
  28.8 6.4 %convert_multiply_fusion = (f32[1,256,2048]{2,1,0:T(8,128)}, f32[1,256,2048]{2,1,0:T(8,128)}) fusion(f32[1,256,2048]{2,1,0:T(8,128)} %copy.219, bf16[1,256,2048]{2,1,0:T(8,128)(2,1)S(1)} %copy-done.3, f32[1,256,2048]{2,1,0:T(8,128)} %copy.209, f32[1,256,2048]{2,1,0:T(8,128)} %copy.208), kind=kLoop, calls=%fused_computation.45 | loop fusion | flops 2097152 | bytes 11534336 | tf_op jit(solution)/shard_map/mul | solution.py:88
  35.2 2.9 copy.220
  38.2 3.7 fusion.55
  42.0 1.7 copy.211
  43.7 23.0 %all-gather = f32[32,32,1]{1,2,0:T(1,128)S(1)} all-gather(f32[1,32,1]{1,2,0:T(1,128)S(1)} %get-tuple-element.586), channel_id=2, replica_groups=mesh['rec'=4,'tm'=32] {'tm'}, dimensions={0}, use_global_device_ids=true | all-gather | bytes 4224 | tf_op jit(solution)/shard_map/all_gather | solution.py:13
  67.7 14.5 %fusion.9 = (f32[32,256]{1,0:T(8,128)}, f32[32,256]{1,0:T(8,128)S(1)}, f32[256,256]{1,0:T(8,128)S(1)}) fusion(f32[256,256]{1,0:T(8,128)S(1)} %fusion.58, f32[32,256]{1,0:T(8,128)S(1)} %copy.205, pred[256,256]{1,0:T(8,128)(4,1)S(1)} %iota_compare_fusion, f32[32,64,256]{2,1,0:T(8,128)} %bitcast.230, f32[256,32,64]{0,2,1:T(8,128)} %bitcast.239, ...), kind=kOutput, calls=%fused_computation.14 | convolution fusion | flops 1634123776 | bytes 4915200 | tf_op jit(solution)/shard_map/transpose(jvp())/while/body/eval_jaxpr/hij,jhp->ihp/dot_general | solution.py:36
  82.3 1.5 copy.225
  84.6 1.5 mul.344
  86.1 2.9 copy.215
  89.1 2.9 copy.210
  92.1 43.2 %all-gather.6.cloned.1.call-done = f32[1024,64,128]{2,1,0:T(8,128)} async-done(((f32[32,64,128]{2,1,0:T(8,128)}), f32[1024,64,128]{2,1,0:T(8,128)}) %all-gather.6.cloned.1.call-update) | async-done | bytes 33554448 | tf_op jit(solution)/shard_map/all_gather | solution.py:13
  135.3 23.7 %rev.7 = f32[32,1,32,64,128]{4,3,2,1,0:T(8,128)} reverse(f32[32,1,32,64,128]{4,3,2,1,0:T(8,128)} %bitcast.228), dimensions={0} | reverse | bytes 67108864 | tf_op jit(solution)/shard_map/rev | solution.py:15
  159.0 91.8 %all-gather.8.cloned.1.call-done = f32[1024,64,128]{2,1,0:T(8,128)} async-done(((f32[32,64,128]{2,1,0:T(8,128)}), f32[1024,64,128]{2,1,0:T(8,128)}) %all-gather.8.cloned.1.call-update) | async-done | bytes 33554448 | tf_op jit(solution)/shard_map/all_gather | solution.py:13
  250.7 46.5 %while.22 = (s32[]{:T(128)}, f32[1,32,64,128]{3,2,1,0:T(8,128)S(1)}, s32[]{:T(128)}, f32[32,1,32]{2,1,0:T(1,128)S(1)}, f32[32,1,32,64,128]{4,3,2,1,0:T(8,128)}, /*index=5*/s32[]{:T(128)}, s32[]{:T(128)}) while((s32[]{:T(128)}, f32[1,32,64,128]{3,2,1,0:T(8,128)S(1)}, s32[]{:T(128)}, f32[32,1,32]{2,1,0:T(1,128)S(1)}, ...), condition=%wide.region_8.9_spmd.clone, body=%wide.region_7.8_spmd.clone.sunk | while | flops 1048580 | bytes 3146217 | solution.py:25
  252.2 1.5 fusion.84
  253.7 1.5 fusion.84
  255.2 1.5 fusion.84
  256.7 1.5 fusion.84
  258.2 1.5 fusion.84
  271.8 1.5 fusion.84
  273.3 1.5 fusion.84
  274.8 1.5 fusion.84
  276.3 1.5 fusion.84
  277.8 1.5 fusion.84
  297.3 2.7 fusion.23
  300.1 10.8 %fusion.21 = bf16[256,32,64]{0,2,1:T(8,128)(2,1)S(1)} fusion(f32[32,64,256]{2,1,0:T(8,128)S(1)} %get-tuple-element.590, f32[256,32,64]{0,2,1:T(8,128)S(1)} %bitcast.241, f32[256,256]{1,0:T(8,128)S(1)} %copy-done.12, f32[32,256]{1,0:T(8,128)S(1)} %copy-done.17, pred[256,256]{1,0:T(8,128)(4,1)S(1)} %copy-done.15, f32[32]{0:T(128)S(1)} %copy-done.22, ...), kind=kOutput, calls=%fused_computation.27 | convolution fusion | flops 1622147072 | bytes 5668992 | tf_op jit(solution)/shard_map/jvp()/while/body/eval_jaxpr/hij,jhp->ihp/dot_general | solution.py:36
  310.9 4.5 fusion.48
  315.4 66.8 %while.21 = (s32[]{:T(128)}, f32[1,32,64,128]{3,2,1,0:T(8,128)S(1)}, s32[]{:T(128)}, f32[32,1,32]{2,1,0:T(1,128)}, f32[32,1,32,64,128]{4,3,2,1,0:T(8,128)}, /*index=5*/s32[]{:T(128)}, s32[]{:T(128)}) while((s32[]{:T(128)}, f32[1,32,64,128]{3,2,1,0:T(8,128)S(1)}, s32[]{:T(128)}, f32[32,1,32]{2,1,0:T(1,128)}, ...), condition=%wide.region_3.4_spmd.clone, body=%wide.region_2.3_spmd.clone.sunk | while | flops 1048580 | bytes 3146217 | solution.py:25
  322.7 1.5 fusion.83
  324.8 1.5 fusion.83
  327.0 1.5 fusion.83
  329.1 1.5 fusion.83
  331.2 1.5 fusion.83
  333.4 1.5 fusion.83
  335.6 1.5 fusion.83
  337.8 1.5 fusion.83
  340.0 1.5 fusion.83
  342.2 1.5 fusion.83
  344.4 1.5 fusion.83
  346.5 1.5 fusion.83
  348.7 1.5 fusion.83
  350.9 1.5 fusion.83
  353.1 1.5 fusion.83
  363.6 1.6 fusion.83
  370.0 1.5 fusion.83
  372.1 1.5 fusion.83
  374.3 1.5 fusion.83
  376.4 1.5 fusion.83
  378.6 1.5 fusion.83
  383.9 10.4 %fusion.24 = (f32[256,32]{0,1:T(8,128)}, f32[256,32]{0,1:T(8,128)S(1)}, f32[256,32,64]{0,2,1:T(8,128)}) fusion(f32[32,64,256]{2,1,0:T(8,128)S(1)} %fusion.43, f32[256,32,64]{0,2,1:T(8,128)} %bitcast.240, f32[256,32]{0,1:T(8,128)S(1)} %bitcast.247, f32[32,64,256]{2,1,0:T(8,128)S(1)} %bitcast.231, f32[256,256]{1,0:T(8,128)S(1)} %copy-done.13, ...), kind=kOutput, calls=%fused_computation.36 | convolution fusion | flops 1623179264 | bytes 8880128 | tf_op jit(solution)/shard_map/transpose(jvp())/while/body/eval_jaxpr/hij,jhp->ihp/dot_general | solution.py:36
  398.6 2.5 reduce-window.26
  401.4 2.9 copy.207
  404.3 6.4 %fusion.22 = (f32[2048]{0:T(1024)S(1)}, f32[256,2048]{1,0:T(8,128)}, f32[1,256,2048]{2,1,0:T(8,128)}) fusion(f32[256,2048]{1,0:T(8,128)} %fusion.50, bf16[1,256,2048]{2,1,0:T(8,128)(2,1)} %param.12, f32[256,2048]{1,0:T(8,128)} %copy.215, f32[256,2048]{1,0:T(8,128)} %copy.207, f32[2048]{0:T(1024)S(1)} %mul.322), kind=kLoop, calls=%fused_computation.29 | loop fusion | flops 3143680 | bytes 11550720 | tf_op jit(solution)/shard_map/transpose(jvp())/reduce_sum | solution.py:67
  410.9 3.0 copy.216
  414.8 5.0 %convolution_bitcast_fusion = f32[256,128]{1,0:T(8,128)S(1)} fusion(f32[256,32,64]{0,2,1:T(8,128)} %bitcast.233, f32[1,32,64,128]{3,2,1,0:T(8,128)S(1)} %get-tuple-element.448), kind=kOutput, calls=%fused_computation.46 | convolution fusion | flops 805306368 | bytes 3276800 | tf_op jit(solution)/shard_map/transpose(jvp(kin,khpn->kihp))/dot_general | solution.py:64
  419.8 5.0 %convolution_bitcast_fusion.1 = f32[256,128]{1,0:T(8,128)S(1)} fusion(f32[256,32,64]{0,2,1:T(8,128)} %bitcast.232, f32[1,32,64,128]{3,2,1,0:T(8,128)S(1)} %get-tuple-element.447), kind=kOutput, calls=%fused_computation.47 | convolution fusion | flops 805306368 | bytes 3276800 | tf_op jit(solution)/shard_map/transpose(jvp())/while/body/eval_jaxpr/jhp,jn->hpn/dot_general | solution.py:41
  424.9 64.9 %all-reduce.2 = (f32[32]{0:T(128)}, f32[32]{0:T(128)}) all-reduce(f32[32]{0:T(128)S(1)} %negate_multiply_fusion, f32[32]{0:T(128)S(1)} %reduce_sum.152), channel_id=1, replica_groups=mesh['rec'=4,'tm'=32] {'rec','tm'}, use_global_device_ids=true, to_apply=%region_19.20 | all-reduce | flops 64 | bytes 512 | tf_op jit(solution)/shard_map/psum | solution.py:122
  491.8 1.7 copy.263
  (215 shorter events, 82.6 us)
Async XLA Ops:
  7.2 2.5 copy-start
  7.2 128.1 %all-gather.6.cloned.1.call-start = ((), (), s32[]{:S(2)}) async-start(), calls=%async_computation.3 | async-start | bytes 34603008 | tf_op jit(solution)/shard_map/all_gather | solution.py:13
  7.9 11.0 %copy-start.18 = (f32[32]{0:T(128)}, f32[32]{0:T(128)S(1)}, u32[]{:S(2)}) copy-start(f32[32]{0:T(128)S(1)} %exponential_negate_fusion) | copy-start | bytes 388
  14.5 2.0 copy-start.6
  16.4 2.3 copy-start.1
  16.5 2.3 copy-start.7
  18.7 232.0 %all-gather.8.cloned.1.call-start = ((), (), s32[]{:S(2)}) async-start(), calls=%async_computation.4 | async-start | bytes 34603008 | tf_op jit(solution)/shard_map/all_gather | solution.py:13
  19.9 2.3 copy-start.20
  25.8 3.0 copy-start.3
  35.2 2.9 copy-start.5
  41.9 378.0 %reduce-scatter.2.cloned.1.call-start = ((), (), s32[]{:S(2)}) async-start(), calls=%async_computation.1 | async-start | bytes 8650752 | tf_op jit(solution)/shard_map/reduce_scatter | solution.py:124
  42.0 25.7 %copy-start.16 = (f32[32,256]{1,0:T(8,128)}, f32[32,256]{1,0:T(8,128)S(1)}, u32[]{:S(2)}) copy-start(f32[32,256]{1,0:T(8,128)S(1)} %copy.205) | copy-start | bytes 98308
  67.5 14.8 %copy-start.14 = (pred[256,256]{1,0:T(8,128)(4,1)}, pred[256,256]{1,0:T(8,128)(4,1)S(1)}, u32[]{:S(2)}) copy-start(pred[256,256]{1,0:T(8,128)(4,1)S(1)} %iota_compare_fusion) | copy-start | bytes 196612
  67.7 14.6 %copy-start.11 = (f32[256,256]{1,0:T(8,128)}, f32[256,256]{1,0:T(8,128)S(1)}, u32[]{:S(2)}) copy-start(f32[256,256]{1,0:T(8,128)S(1)} %fusion.58) | copy-start | bytes 786436
  86.0 2.9 copy-start.22
  297.3 2.8 copy-start.4
  297.3 2.8 copy-start.12
  297.3 2.8 copy-start.15
  297.3 2.8 copy-start.17
  315.4 176.4 %all-reduce.5.cloned.1.call-start = ((), (), s32[]{:S(2)}) async-start(), calls=%async_computation.2 | async-start | bytes 524288 | tf_op jit(solution)/shard_map/psum | solution.py:130
  382.2 1.6 copy-start.2
  382.3 1.6 copy-start.13
  383.9 12.0 %copy-start.21 = (f32[32]{0:T(128)S(1)}, f32[32]{0:T(128)}, u32[]{:S(2)}) copy-start(f32[32]{0:T(128)} %copy-done.20) | copy-start | bytes 388
  395.9 0.9 copy-start.8
  395.9 1.0 copy-start.9
  395.9 1.0 copy-start.10
  410.9 3.1 copy-start.19
  410.9 3.9 copy-start.23
Sparse Core Ops, SparseCore 0:
  18.8 116.4 all-gather.5
  137.6 113.1 all-gather.7
  315.5 92.0 reduce-scatter.1
  420.0 40.9 all-reduce.4
where the time goes:
time: 504 us; the launch traced here: 500 us
  waiting for transfers between devices  135 us (27%)
  other arithmetic  112 us (22%)
  blocking collectives  88 us (17%)
  local copies, waits for them, and re-layouts  82.2 us (16%)
  matrix products  66.7 us (13%)
  between operations  14.2 us (3%)
    all_gather x2, waiting for transfers between devices, prefix(): pieces = jax.tree.map(lambda part: lax.all_gather(part, axis), value)  135 us
    select_n x62, other arithmetic, hop(): jnp.where(position < mine, new, old)  91.5 us
    psum x1, blocking collectives, local(): grad_decay, grad_skip = lax.psum((decay_part, skip_part), ('rec', 'tm'))  64.9 us
    dot_general x3, matrix products, block_terms(): jnp.einsum('hij,jhp->ihp', decay_mat * scores[None], scaled, precision=la...  35.7 us
    rev x2, local copies, waits for them, and re-layouts, prefix(): pieces = jax.tree.map(lambda part: part[::-1], pieces)  24.3 us
    all_gather x1, blocking collectives, prefix(): pieces = jax.tree.map(lambda part: lax.all_gather(part, axis), value)  23 us
    mul x62, local copies, waits for them, and re-layouts, chain(): late_decay[:, :, None, None] * early_state + late_state  20.1 us
  transfers between devices with their start and end apart: 4, of which 2 were waited for; matrix products, arithmetic and copies ran while one was open for 37% of the time, Pallas kernels for 0%

commit v1 on v0

v1 whole, which is shorter than its diff:
```python
import jax
import jax.numpy as jnp
from jax import lax
from jax.experimental import pallas as pl
from jax.experimental.pallas import tpu as pltpu
from jax.sharding import PartitionSpec as P

HEADS = 32
WIDTH = 64
PAIR = 2 * WIDTH
STATE = 128
SPAN = 256
INNER = HEADS * WIDTH
MODEL = 1024
CHIPS = 16
LOG2E = 1.4426950408889634
MESH = pl.DeviceIdType.MESH
HIGHEST = lax.Precision.HIGHEST
F32 = jnp.float32
BF16 = jnp.bfloat16


def nn(a, b, precision=None):
    return lax.dot_general(
        a, b, (((1,), (0,)), ((), ())), precision=precision, preferred_element_type=F32
    )


def nt(a, b, precision=None):
    return lax.dot_general(
        a, b, (((1,), (1,)), ((), ())), precision=precision, preferred_element_type=F32
    )


def column(row):
    i = lax.broadcasted_iota(jnp.int32, (HEADS, HEADS), 0)
    j = lax.broadcasted_iota(jnp.int32, (HEADS, HEADS), 1)
    whole = jnp.broadcast_to(row, (HEADS, HEADS))
    return jnp.sum(jnp.where(i == j, whole, 0.0), axis=1, keepdims=True)


def running_sums(dt, rate):
    s = lax.broadcasted_iota(jnp.int32, (SPAN, SPAN), 0)
    t = lax.broadcasted_iota(jnp.int32, (SPAN, SPAN), 1)
    upto = jnp.where(s <= t, 1.0, 0.0).astype(F32)
    return nn(-rate * dt, upto, HIGHEST)


def two_rows(ref, k):
    top = jnp.broadcast_to(ref[pl.ds(2 * k, 1), :], (WIDTH, ref.shape[1]))
    low = jnp.broadcast_to(ref[pl.ds(2 * k + 1, 1), :], (WIDTH, ref.shape[1]))
    return jnp.concatenate([top, low], axis=0)


def split(v):
    high = v.astype(BF16)
    return high, (v - high.astype(F32)).astype(BF16)


def entry_kernel(
    x_ref, k_ref, q_ref, dt_ref, dl_ref, w_ref, og_ref,
    t_ref, e_ref, d_ref, gt_ref, xt_ref, wrow, erow, drow, gbuf,
):
    dt = dt_ref[...]
    run = running_sums(dt, jnp.exp(column(dl_ref[...])))
    end = run[:, SPAN - 1 :]
    wrow[...] = jnp.exp(end - run) * dt
    erow[...] = jnp.exp(run)
    drow[...] = jnp.broadcast_to(jnp.exp(end), (HEADS, STATE))
    for h in range(HEADS):
        d_ref[h] = jnp.broadcast_to(drow[h : h + 1, :], (8, STATE))

    def chunk(m, carry):
        rows = pl.ds(pl.multiple_of(m * 512, 512), 512)
        gbuf[...] = nt(w_ref[rows, :], og_ref[...])
        for i in range(4):
            k = m * 4 + i
            at = pl.ds(pl.multiple_of(k * PAIR, PAIR), PAIR)
            g = gbuf[i * PAIR : (i + 1) * PAIR, :]
            gt_ref[at, :] = g
            high, low = split(g * two_rows(erow, k))
            e_ref[at, :] = nn(high, q_ref[...]) + nn(low, q_ref[...])
            xt = x_ref[:, at].T
            xt_ref[at, :] = xt
            high, low = split(xt.astype(F32) * two_rows(wrow, k))
            t_ref[at, :] = nn(high, k_ref[...]) + nn(low, k_ref[...])
        return carry

    lax.fori_loop(0, 4, chunk, 0)


def scan_kernel(
    t_ref, e_ref, d_ref, s_ref, ds_ref,
    tp, ep, dp, up, got, back, home, give_s, give_d,
    core_send, core_recv, out_send, out_recv, in_send, in_recv,
):
    rec, me = lax.axis_index("rec"), lax.axis_index("tm")
    c, g = lax.rem(me, 2), lax.div(me, 2)
    partner = me + 1 - 2 * c

    def peer(d):
        return lax.rem(g + d, CHIPS)

    barrier = pltpu.get_barrier_semaphore()
    pl.semaphore_signal(barrier, inc=1, device_id=(rec, partner), device_id_type=MESH)
    for d in range(1, CHIPS):
        pl.semaphore_signal(barrier, inc=1, device_id=(rec, peer(d) * 2 + c), device_id_type=MESH)
    pl.semaphore_wait(barrier, CHIPS)

    def core_copy(src, dst, i):
        return pltpu.make_async_remote_copy(
            src_ref=src, dst_ref=dst, send_sem=core_send.at[i], recv_sem=core_recv.at[i],
            device_id=(rec, partner), device_id_type=MESH,
        )

    mine, theirs = pl.ds(c * CHIPS, CHIPS), pl.ds((1 - c) * CHIPS, CHIPS)
    swaps = [
        core_copy(d_ref, dp, 0),
        core_copy(t_ref.at[theirs], tp, 1),
        core_copy(e_ref.at[theirs], ep, 2),
    ]
    for s in swaps:
        s.start()
    for s in swaps:
        s.wait()
    first = c == 0

    def both(a, b):
        return jnp.where(first, a, b), jnp.where(first, b, a)

    def combine(i, carry):
        h = c * CHIPS + i
        d0, d1 = both(d_ref[h], dp[h])
        t0, t1 = both(t_ref[h], tp[i])
        e0, e1 = both(e_ref[h], ep[i])
        up[i, 0:8] = d1[None] * t0 + t1
        up[i, 8:16] = e0 + d0[None] * e1
        up[i, 16] = d0 * d1
        return carry

    lax.fori_loop(0, CHIPS, combine, 0)

    def spread(src, dst, d, send, recv):
        return pltpu.make_async_remote_copy(
            src_ref=src.at[peer(d)], dst_ref=dst.at[g], send_sem=send.at[d], recv_sem=recv.at[d],
            device_id=(rec, peer(d) * 2 + c), device_id_type=MESH,
        )

    outs = [spread(up, got, d, out_send, out_recv) for d in range(1, CHIPS)]
    for o in outs:
        o.start()
    got[g] = up[g]
    for o in outs:
        o.wait()
    carried = jnp.zeros((8, 8, STATE), F32)
    for i in range(CHIPS):
        back[i, 0:8] = carried
        carried = got[i, 16][None] * carried + got[i, 0:8]
    carried = jnp.zeros((8, 8, STATE), F32)
    for i in range(CHIPS - 1, -1, -1):
        back[i, 8:16] = carried
        carried = got[i, 16][None] * carried + got[i, 8:16]
    ins = [spread(back, home, d, in_send, in_recv) for d in range(1, CHIPS)]
    for o in ins:
        o.start()
    home[g] = back[g]
    for o in ins:
        o.wait()

    def finish(i, carry):
        h = c * CHIPS + i
        d0, d1 = both(d_ref[h], dp[h])
        t0, t1 = both(t_ref[h], tp[i])
        e0, e1 = both(e_ref[h], ep[i])
        s0 = home[i, 0:8]
        s1 = d0[None] * s0 + t0
        b1 = home[i, 8:16]
        b0 = d1[None] * b1 + e1
        s_ref[h], give_s[i] = both(s0, s1)
        ds_ref[h], give_d[i] = both(b0, b1)
        return carry

    lax.fori_loop(0, CHIPS, finish, 0)
    gives = [core_copy(give_s, s_ref.at[mine], 3), core_copy(give_d, ds_ref.at[mine], 4)]
    for s in gives:
        s.start()
    for s in gives:
        s.wait()


def inner_kernel(
    x_ref, xt_ref, gt_ref, k_ref, q_ref, dt_ref, dl_ref, sk_ref, s_ref, ds_ref,
    gv_ref, gk_ref, gq_ref, gs_ref, sm_ref, st_ref,
    run2, crow, wrow, erow, skrow, scores, acc, qacc, kacc, frow, rrow, urow, xrow, vrow,
):
    dt = dt_ref[...]
    rate = jnp.exp(column(dl_ref[...]))
    run = running_sums(dt, rate)
    end = run[:, SPAN - 1 :]
    run2[...] = run * LOG2E
    crow[...] = run * LOG2E - jnp.log2(dt)
    wrow[...] = jnp.exp(end - run) * dt
    erow[...] = jnp.exp(run)
    skrow[...] = jnp.broadcast_to(column(sk_ref[...]), (HEADS, SPAN))
    j = lax.broadcasted_iota(jnp.int32, (SPAN, SPAN), 0)
    i = lax.broadcasted_iota(jnp.int32, (SPAN, SPAN), 1)
    causal = j <= i
    scores[...] = jnp.where(causal, nt(k_ref[...], q_ref[...]), 0.0)
    acc[...] = jnp.zeros_like(acc)
    qacc[...] = jnp.zeros_like(qacc)
    kacc[...] = jnp.zeros_like(kacc)
    half = SPAN // 2

    def pair(k, carry):
        at = pl.ds(pl.multiple_of(k * PAIR, PAIR), PAIR)
        xp = x_ref[:, at]
        xt = xt_ref[at, :]
        gf = gt_ref[at, :]
        gh, gl = split(gf)
        x2 = jnp.concatenate([xp, xp], axis=1)
        y_parts, yl_parts, dx_parts = [], [], []
        for e in range(2):
            row = run2[pl.ds(2 * k + e, 1), :]
            crow_b = jnp.broadcast_to(crow[pl.ds(2 * k + e, 1), :], (half, SPAN))
            ccol = crow_b.T
            d00 = jnp.exp2(jnp.minimum(row[:, :half] - ccol[:half], 2.0))
            d01 = jnp.exp2(row[:, half:] - ccol[:half])
            d11 = jnp.exp2(jnp.minimum(row[:, half:] - ccol[half:], 2.0))
            n00, l00 = split(d00 * scores[:half, :half])
            n01, l01 = split(d01 * scores[:half, half:])
            n11, l11 = split(d11 * scores[half:, half:])
            n10 = jnp.zeros((half, half), BF16)

            def square(a, b, d):
                top = jnp.concatenate([a, b], axis=1)
                return jnp.concatenate([top, jnp.concatenate([n10, d], axis=1)], axis=0)

            n = square(n00, n01, n11)
            part = slice(e * WIDTH, (e + 1) * WIDTH)
            y_parts.append(nn(xt[part], n))
            yl_parts.append(nn(xt[part], square(l00, l01, l11)))
            dx = nt(jnp.concatenate([gh[part], gl[part]], axis=0), n)
            dx_parts.append(dx[:WIDTH] + dx[WIDTH:])
            blank = jnp.zeros((WIDTH, SPAN), BF16)
            if e == 0:
                gz = jnp.concatenate([gh[part], blank, gl[part], blank], axis=0)
            else:
                gz = jnp.concatenate([blank, gh[part], blank, gl[part]], axis=0)
            dn = nn(x2, gz)
            acc[:half, :half] += dn[:half, :half] * d00
            acc[:half, half:] += dn[:half, half:] * d01
            acc[half:, half:] += dn[half:, half:] * d11
        xf = xt.astype(F32)
        wp = two_rows(wrow, k)
        ep = two_rows(erow, k)
        skp = two_rows(skrow, k)
        sp = s_ref[at, :]
        dsp = ds_ref[at, :]
        sh, sl = split(sp)
        dsh, dsl = split(dsp)
        y = jnp.concatenate(y_parts, axis=0) + (nt(sh, q_ref[...]) + nt(sl, q_ref[...])) * ep
        st_ref[at, :] = (y + jnp.concatenate(yl_parts, axis=0) + skp * xf).astype(BF16)
        dxs = (nt(dsh, k_ref[...]) + nt(dsl, k_ref[...])) * wp
        dx = jnp.concatenate(dx_parts, axis=0) + dxs
        gv_ref[:, at] = (dx + skp * gf).T
        ge = (gf * ep).astype(BF16)
        xw = (xf * wp).astype(BF16)
        qacc[...] += nn(sh.T, ge) + nn(sl.T, ge)
        kacc[...] += nn(dsh.T, xw) + nn(dsl.T, xw)
        for ref, value in ((frow, gf * y), (rrow, xf * dx), (urow, xf * dxs), (xrow, gf * xf), (vrow, sp * dsp)):
            for e in range(2):
                ref[pl.ds(2 * k + e, 1), :] = jnp.sum(
                    value[e * WIDTH : (e + 1) * WIDTH], axis=0, keepdims=True
                )
        return carry

    lax.fori_loop(0, HEADS // 2, pair, 0)
    dst = jnp.where(causal, acc[...], 0.0).astype(BF16)
    gk_ref[...] = nn(dst, q_ref[...]) + kacc[...].T
    gq_ref[...] = (nn(k_ref[...].T, dst) + qacc[...]).T
    upto = jnp.where(i <= j, 1.0, 0.0).astype(F32)
    tail = jnp.sum(urow[...], axis=1, keepdims=True)
    tail = tail + jnp.exp(end) * jnp.sum(vrow[...], axis=1, keepdims=True)
    da = nn(frow[...] - rrow[...], upto, HIGHEST) + tail
    gs_ref[...] = rrow[...] / dt - rate * da
    decay = jnp.sum(-rate * dt * da, axis=1, keepdims=True)
    skip = jnp.sum(xrow[...], axis=1, keepdims=True)
    lane = lax.broadcasted_iota(jnp.int32, (HEADS, 128), 1)
    sm_ref[...] = jnp.where(lane == 0, decay, jnp.where(lane == 1, skip, 0.0))


PARTS = ((0, 384, "xyz"), (384, 384, "yzx"), (768, 256, "zxy"))


def weight_kernel(
    st_ref, og_ref, sm_ref, gw_ref, smo_ref,
    f_st, f_og, r_st, r_og, lhs, rhs, dw,
    a0, a1, a2, b0, b1, b2, ra0, ra1, ra2, rb0, rb1, rb2, rc0, rc1, rc2,
    s_core, s_x, s_y, s_z,
    core_send, core_recv, send, recv, s_send, s_recv,
):
    y, me = lax.axis_index("rec"), lax.axis_index("tm")
    c, g = lax.rem(me, 2), lax.div(me, 2)
    x, z = lax.div(g, 4), lax.rem(g, 4)
    partner = me + 1 - 2 * c
    coord = {"x": x, "y": y, "z": z}

    def device(axis, value):
        if axis == "x":
            return (y, (value * 4 + z) * 2 + c)
        if axis == "z":
            return (y, (x * 4 + value) * 2 + c)
        return (value, me)

    def other(axis, d):
        return lax.rem(coord[axis] + d, 4)

    barrier = pltpu.get_barrier_semaphore()
    pl.semaphore_signal(barrier, inc=1, device_id=(y, partner), device_id_type=MESH)
    for axis in "xyz":
        for d in range(1, 4):
            pl.semaphore_signal(
                barrier, inc=1, device_id=device(axis, other(axis, d)), device_id_type=MESH
            )
    pl.semaphore_wait(barrier, 10)

    def core_copy(src, dst, n):
        return pltpu.make_async_remote_copy(
            src_ref=src, dst_ref=dst, send_sem=core_send.at[n], recv_sem=core_recv.at[n],
            device_id=(y, partner), device_id_type=MESH,
        )

    f_og[...] = og_ref[...].astype(F32)
    f_st[...] = st_ref[:, 1 - c].astype(F32)
    s_core[c] = sm_ref[...]
    swaps = [core_copy(f_og, r_og, 0), core_copy(f_st, r_st, 1), core_copy(s_core.at[c], s_core.at[c], 2)]
    for s in swaps:
        s.start()
    rhs[:SPAN] = og_ref[...]
    lhs[:, :SPAN] = st_ref[:, c].reshape(CHIPS * WIDTH, SPAN)
    for s in swaps:
        s.wait()
    rhs[SPAN:] = r_og[...].astype(BF16)
    lhs[:, SPAN:] = r_st[...].astype(BF16).reshape(CHIPS * WIDTH, SPAN)

    def product(m, carry):
        rows = pl.ds(pl.multiple_of(m * SPAN, SPAN), SPAN)
        dw[m] = nn(lhs[rows, :], rhs[...]).reshape(4, 4, 16, MODEL)
        return carry

    lax.fori_loop(0, 4, product, 0)

    def reach(axis, d, src, dst, n, sends=send, recvs=recv):
        return pltpu.make_async_remote_copy(
            src_ref=src, dst_ref=dst, send_sem=sends.at[n, d - 1], recv_sem=recvs.at[n, d - 1],
            device_id=device(axis, other(axis, d)), device_id_type=MESH,
        )

    def pick(dims, axis, value):
        return tuple(value if n == axis else slice(None) for n in dims)

    def reduce_start(p, phase, src, dims, axis, dst):
        copies = []
        for d in range(1, 4):
            at = pick(dims, axis, other(axis, d))
            if phase == 0:
                at = at + (slice(None), pl.ds(PARTS[p][0], PARTS[p][1]))
            copies.append(reach(axis, d, src.at[at], dst.at[d - 1], phase * 3 + p))
        for cp in copies:
            cp.start()
        return copies

    sums_a, sums_b = (a0, a1, a2), (b0, b1, b2)
    recv_a, recv_b, recv_c = (ra0, ra1, ra2), (rb0, rb1, rb2), (rc0, rc1, rc2)
    dims = "xzy"
    first = [
        reduce_start(p, 0, dw, dims, order[0], recv_a[p]) for p, (_, _, order) in enumerate(PARTS)
    ]
    small = s_core[0] + s_core[1]
    second = []
    for n, (axis, buf) in enumerate((("x", s_x), ("y", s_y), ("z", s_z))):
        buf[coord[axis]] = small
        copies = [
            reach(axis, d, buf.at[coord[axis]], buf.at[coord[axis]], n, s_send, s_recv) for d in range(1, 4)
        ]
        for cp in copies:
            cp.start()
        for cp in copies:
            cp.wait()
        small = (buf[0] + buf[1]) + (buf[2] + buf[3])
    smo_ref[...] = small
    for p, (low, wide, order) in enumerate(PARTS):
        for cp in first[p]:
            cp.wait()
        at = pick(dims, order[0], coord[order[0]]) + (slice(None), pl.ds(low, wide))
        got = recv_a[p]
        sums_a[p][...] = (dw[at] + got[0]) + (got[1] + got[2])
        rest = dims.replace(order[0], "")
        second.append(reduce_start(p, 1, sums_a[p], rest, order[1], recv_b[p]))
    third = []
    for p, (low, wide, order) in enumerate(PARTS):
        for cp in second[p]:
            cp.wait()
        rest = dims.replace(order[0], "")
        at = pick(rest, order[1], coord[order[1]])
        got = recv_b[p]
        sums_b[p][...] = (sums_a[p][at] + got[0]) + (got[1] + got[2])
        third.append(reduce_start(p, 2, sums_b[p], order[2], order[2], recv_c[p]))
    last = []
    rows = pl.ds(pl.multiple_of(y * 16, 16), 16)
    for p, (low, wide, order) in enumerate(PARTS):
        for cp in third[p]:
            cp.wait()
        got = recv_c[p]
        cols = pl.ds(low, wide)
        gw_ref[rows, cols] = (sums_b[p][coord[order[2]]] + got[0]) + (got[1] + got[2])
        copies = [
            reach("y", d, gw_ref.at[rows, cols], gw_ref.at[rows, cols], 9 + p) for d in range(1, 4)
        ]
        for cp in copies:
            cp.start()
        last.extend(copies)
    for cp in last:
        cp.wait()


def vmem(count):
    return [pl.BlockSpec(memory_space=pltpu.VMEM)] * count


def sds(shape, dtype=F32):
    return jax.ShapeDtypeStruct(shape, dtype)


def local(token_values, write_keys, read_queries, step_sizes, decay_log, skip_gain, out_weight, out_grad):
    x, k, q, dt, og = token_values[0], write_keys[0], read_queries[0], step_sizes[0], out_grad[0]
    dl, sk = decay_log.reshape(1, HEADS), skip_gain.reshape(1, HEADS)
    limit = 48 * 1024 * 1024
    t, e, d, gt, xt = pl.pallas_call(
        entry_kernel,
        out_shape=(
            sds((INNER, STATE)), sds((INNER, STATE)), sds((HEADS, 8, STATE)),
            sds((INNER, SPAN)), sds((INNER, SPAN), BF16),
        ),
        in_specs=vmem(7),
        out_specs=tuple(vmem(5)),
        scratch_shapes=[
            pltpu.VMEM((HEADS, SPAN), F32), pltpu.VMEM((HEADS, SPAN), F32), pltpu.VMEM((HEADS, STATE), F32),
            pltpu.VMEM((512, SPAN), F32),
        ],
        compiler_params=pltpu.CompilerParams(vmem_limit_bytes=limit),
        name="entry",
    )(x, k, q, dt, dl, out_weight, og)
    grid = (HEADS, 8, 8, STATE)
    s_in, ds_out = pl.pallas_call(
        scan_kernel,
        out_shape=(sds(grid), sds(grid)),
        in_specs=vmem(3),
        out_specs=tuple(vmem(2)),
        scratch_shapes=[
            pltpu.VMEM((CHIPS, 8, 8, STATE), F32),
            pltpu.VMEM((CHIPS, 8, 8, STATE), F32),
            pltpu.VMEM((HEADS, 8, STATE), F32),
            pltpu.VMEM((CHIPS, 17, 8, STATE), F32),
            pltpu.VMEM((CHIPS, 17, 8, STATE), F32),
            pltpu.VMEM((CHIPS, 16, 8, STATE), F32),
            pltpu.VMEM((CHIPS, 16, 8, STATE), F32),
            pltpu.VMEM((CHIPS, 8, 8, STATE), F32),
            pltpu.VMEM((CHIPS, 8, 8, STATE), F32),
            pltpu.SemaphoreType.DMA((5,)), pltpu.SemaphoreType.DMA((5,)),
            pltpu.SemaphoreType.DMA((CHIPS,)), pltpu.SemaphoreType.DMA((CHIPS,)),
            pltpu.SemaphoreType.DMA((CHIPS,)), pltpu.SemaphoreType.DMA((CHIPS,)),
        ],
        compiler_params=pltpu.CompilerParams(
            vmem_limit_bytes=limit, collective_id=0, has_side_effects=True
        ),
        name="scan",
    )(t.reshape(grid), e.reshape(grid), d)
    row = pltpu.VMEM((HEADS, SPAN), F32)
    gv, gk, gq, gs, small, stored = pl.pallas_call(
        inner_kernel,
        out_shape=(
            sds((SPAN, INNER)), sds((SPAN, STATE)), sds((SPAN, STATE)), sds((HEADS, SPAN)),
            sds((HEADS, 128)), sds((INNER, SPAN), BF16),
        ),
        in_specs=vmem(10),
        out_specs=tuple(vmem(6)),
        scratch_shapes=[
            row, row, row, row, row,
            pltpu.VMEM((SPAN, SPAN), F32), pltpu.VMEM((SPAN, SPAN), F32),
            pltpu.VMEM((STATE, SPAN), F32), pltpu.VMEM((STATE, SPAN), F32),
            row, row, row, row, pltpu.VMEM((HEADS, STATE), F32),
        ],
        compiler_params=pltpu.CompilerParams(vmem_limit_bytes=limit),
        name="inner",
    )(x, xt, gt, k, q, dt, dl, sk, s_in.reshape(INNER, STATE), ds_out.reshape(INNER, STATE))
    dma = pltpu.SemaphoreType.DMA
    wides = [w for _, w, _ in PARTS]
    gw, small = pl.pallas_call(
        weight_kernel,
        out_shape=(sds((64, MODEL)), sds((HEADS, 128))),
        in_specs=vmem(3),
        out_specs=tuple(vmem(2)),
        scratch_shapes=[
            pltpu.VMEM((CHIPS, WIDTH, SPAN), F32), pltpu.VMEM((SPAN, MODEL), F32),
            pltpu.VMEM((CHIPS, WIDTH, SPAN), F32), pltpu.VMEM((SPAN, MODEL), F32),
            pltpu.VMEM((CHIPS * WIDTH, 2 * SPAN), BF16), pltpu.VMEM((2 * SPAN, MODEL), BF16),
            pltpu.VMEM((4, 4, 4, 16, MODEL), F32),
            *[pltpu.VMEM((4, 4, 16, w), F32) for w in wides],
            *[pltpu.VMEM((4, 16, w), F32) for w in wides],
            *[pltpu.VMEM((3, 4, 4, 16, w), F32) for w in wides],
            *[pltpu.VMEM((3, 4, 16, w), F32) for w in wides],
            *[pltpu.VMEM((3, 16, w), F32) for w in wides],
            pltpu.VMEM((2, HEADS, 128), F32),
            *[pltpu.VMEM((4, HEADS, 128), F32)] * 3,
            dma((3,)), dma((3,)), dma((12, 3)), dma((12, 3)), dma((3, 3)), dma((3, 3)),
        ],
        compiler_params=pltpu.CompilerParams(
            vmem_limit_bytes=limit, collective_id=1, has_side_effects=True
        ),
        name="weight",
    )(stored.reshape(CHIPS, 2, WIDTH, SPAN), og, small)
    return gv[None], gk[None], gq[None], gs[None], small[:, 0], small[:, 1], gw


def solution(mesh):
    by_time = P("rec", "tm", None)
    by_head = P("rec", None, "tm")
    return jax.shard_map(
        local,
        mesh=mesh,
        in_specs=(by_time, by_time, by_time, by_head, P(), P(), P(), by_time),
        out_specs=(by_time, by_time, by_time, by_head, P(), P(), P("tm", None)),
        check_vma=False,
    )
```

time: 504 us -> 131 us (0.26)
  waiting for transfers between devices: 135 us -> 0 us
  Pallas kernels: 0 us -> 123 us
  other arithmetic: 112 us -> 0 us
  blocking collectives: 88 us -> 0 us
  local copies, waits for them, and re-layouts: 82.2 us -> 6.77 us
  matrix products: 66.7 us -> 0 us
  between operations: 14.2 us -> 0.69 us
    all_gather x2 -> x0, waiting for transfers between devices: 135 us -> none  [prefix(): pieces = jax.tree.map(lambda part: lax.all_gather(part, axis), value)]
    pallas_call x0 -> x4, Pallas kernels: none -> 123 us  [the longest x1 54.6 us: local(): pl.pallas_call(weight_kernel, out_shape=(sds((64, MODEL)), sds((HEADS, 12...]
    select_n x62 -> x0, other arithmetic: 91.5 us -> none  [hop(): jnp.where(position < mine, new, old)]
    dot_general x14 -> x0, matrix products: 66.7 us -> none  [the longest x3 35.7 us: block_terms(): jnp.einsum('hij,jhp->ihp', decay_mat * scores[None], scaled, precision=la...]
    psum x1 -> x0, blocking collectives: 64.9 us -> none  [local(): grad_decay, grad_skip = lax.psum((decay_part, skip_part), ('rec', 'tm'))]
    mul x77 -> x0, local copies, waits for them, and re-layouts: 44.9 us -> none  [the longest x62 20.1 us: chain(): late_decay[:, :, None, None] * early_state + late_state]
    rev x2 -> x0, local copies, waits for them, and re-layouts: 24.3 us -> none  [prefix(): pieces = jax.tree.map(lambda part: part[::-1], pieces)]
    all_gather x1 -> x0, blocking collectives: 23 us -> none  [prefix(): pieces = jax.tree.map(lambda part: lax.all_gather(part, axis), value)]
  transfers between devices with their start and end apart: 4 -> 0, of which waited for: 2 -> 0; matrix products, arithmetic and copies ran while one was open for 37% -> 0% of each run, Pallas kernels for 0% -> 0%
where the time goes in v1:
time: 131 us; the launch traced here: 130 us
  Pallas kernels  123 us (94%)
  local copies, waits for them, and re-layouts  6.77 us (5%)
    pallas_call x1, Pallas kernels, local(): pl.pallas_call(weight_kernel, out_shape=(sds((64, MODEL)), sds((HEADS, 12...  54.6 us
    pallas_call x1, Pallas kernels, local(): pl.pallas_call(scan_kernel, out_shape=(sds(grid), sds(grid)), in_specs=vm...  45.5 us
    pallas_call x1, Pallas kernels, local(): pl.pallas_call(inner_kernel, out_shape=(sds((SPAN, INNER)), sds((SPAN, ST...  13.9 us
    pallas_call x1, Pallas kernels, local(): pl.pallas_call(entry_kernel, out_shape=(sds((INNER, STATE)), sds((INNER,...  8.9 us
    unnamed x19, local copies, waits for them, and re-layouts  6.07 us

profile of v1, /device:TPU:0, one launch (start us, length us, event | category | flops | bytes accessed | tf_op | source)
XLA Modules:
  0.0 130.2 jit_solution(15682467888841655737)
XLA Ops:
  0.6 0.0 copy-start
  0.6 1.2 copy-done
  1.9 0.0 copy-start.2
  1.9 1.0 copy-done.2
  2.9 0.0 copy-start.4
  2.9 0.8 copy-done.4
  3.7 0.0 copy-start.5
  3.7 0.8 copy-done.5
  4.6 0.0 copy-start.6
  4.6 0.8 copy-done.6
  5.3 0.0 copy-start.7
  5.3 0.7 copy-done.7
  6.0 8.9 %entry.1 = (f32[2048,128]{1,0:T(8,128)S(1)}, f32[2048,128]{1,0:T(8,128)S(1)}, f32[32,8,128]{2,1,0:T(8,128)S(1)}, f32[2048,256]{1,0:T(8,128)}, bf16[2048,256]{1,0:T(8,128)(2,1)S(1)}) custom-call(bf16[256,2048]{1,0:T(8,128)(2,1)S(1)} %bitcast.16, bf16[256,128]{1,0:T(8,128)(2,1)S(1)} %bitcast.25, bf16[256,128]{1,0:T(8,128)(2,1)S(1)} %bitcast.27, ...), custom_call_target="tpu_custom_call" | custom-call | tf_op jit(solution)/shard_map/entry/pallas_call | solution.py:439
  14.9 0.0 copy-start.1
  14.9 0.0 copy-start.8
  14.9 45.5 %scan.1 = (f32[32,8,8,128]{3,2,1,0:T(8,128)S(1)}, f32[32,8,8,128]{3,2,1,0:T(8,128)S(1)}) custom-call(f32[32,8,8,128]{3,2,1,0:T(8,128)S(1)} %bitcast.21, f32[32,8,8,128]{3,2,1,0:T(8,128)S(1)} %bitcast.22, f32[32,8,128]{2,1,0:T(8,128)S(1)} %get-tuple-element.26.d_ref), custom_call_target="tpu_custom_call" | custom-call | tf_op jit(solution)/shard_map/scan/pallas_call | solution.py:455
  60.4 0.0 copy-done.1
  60.4 0.0 copy-done.8
  60.4 0.0 copy-start.3
  60.4 13.9 %inner.1 = (f32[256,2048]{1,0:T(8,128)}, f32[256,128]{1,0:T(8,128)}, f32[256,128]{1,0:T(8,128)}, f32[32,256]{1,0:T(8,128)}, f32[32,128]{1,0:T(8,128)S(1)}, /*index=5*/bf16[2048,256]{1,0:T(8,128)(2,1)S(1)}) custom-call(bf16[256,2048]{1,0:T(8,128)(2,1)S(1)} %bitcast.17, bf16[2048,256]{1,0:T(8,128)(2,1)S(1)} %get-tuple-element.22.xt_ref, ...), custom_call_target="tpu_custom_call" | custom-call | tf_op jit(solution)/shard_map/inner/pallas_call | solution.py:480
  74.3 0.0 copy-done.3
  74.3 54.6 %weight.1 = (f32[64,1024]{1,0:T(8,128)S(1)}, f32[32,128]{1,0:T(8,128)S(1)}) custom-call(bf16[16,2,64,256]{3,2,1,0:T(8,128)(2,1)S(1)} %bitcast.20, bf16[256,1024]{1,0:T(8,128)(2,1)S(1)} %bitcast.19, f32[32,128]{1,0:T(8,128)S(1)} %get-tuple-element.34.sm_ref), custom_call_target="tpu_custom_call" | custom-call | tf_op jit(solution)/shard_map/weight/pallas_call | solution.py:499
  128.8 0.7 slice_reduce_fusion
  129.5 0.7 copy.16
Async XLA Ops:
  0.6 1.2 copy-start
  1.9 1.0 copy-start.2
  2.9 0.8 copy-start.4
  3.7 0.8 copy-start.5
  4.6 0.8 copy-start.6
  5.3 0.7 copy-start.7
  14.9 45.5 %copy-start.1 = (bf16[1,256,2048]{2,1,0:T(8,128)(2,1)S(1)}, bf16[1,256,2048]{2,1,0:T(8,128)(2,1)}, u32[]{:S(2)}) copy-start(bf16[1,256,2048]{2,1,0:T(8,128)(2,1)} %param.8) | copy-start | bytes 3145732
  14.9 45.5 %copy-start.8 = (f32[32]{0:T(128)S(1)}, f32[32]{0:T(128)}, u32[]{:S(2)}) copy-start(f32[32]{0:T(128)} %param.13) | copy-start | bytes 388
  60.4 13.9 %copy-start.3 = (bf16[1,256,1024]{2,1,0:T(8,128)(2,1)S(1)}, bf16[1,256,1024]{2,1,0:T(8,128)(2,1)}, u32[]{:S(2)}) copy-start(bf16[1,256,1024]{2,1,0:T(8,128)(2,1)} %param.15) | copy-start | bytes 1572868

commit v2 on v0

v2 whole, which is shorter than its diff:
```python
import jax
import jax.numpy as jnp
from jax import lax
from jax.experimental import pallas as pl
from jax.experimental.pallas import tpu as pltpu
from jax.sharding import PartitionSpec as P

HEADS = 32
WIDTH = 64
PAIR = 2 * WIDTH
STATE = 128
SPAN = 256
INNER = HEADS * WIDTH
MODEL = 1024
CHIPS = 16
LOG2E = 1.4426950408889634
MESH = pl.DeviceIdType.MESH
HIGHEST = lax.Precision.HIGHEST
F32 = jnp.float32
BF16 = jnp.bfloat16


def nn(a, b, precision=None):
    return lax.dot_general(
        a, b, (((1,), (0,)), ((), ())), precision=precision, preferred_element_type=F32
    )


def nt(a, b, precision=None):
    return lax.dot_general(
        a, b, (((1,), (1,)), ((), ())), precision=precision, preferred_element_type=F32
    )


def column(row):
    i = lax.broadcasted_iota(jnp.int32, (HEADS, HEADS), 0)
    j = lax.broadcasted_iota(jnp.int32, (HEADS, HEADS), 1)
    whole = jnp.broadcast_to(row, (HEADS, HEADS))
    return jnp.sum(jnp.where(i == j, whole, 0.0), axis=1, keepdims=True)


def running_sums(dt, rate):
    s = lax.broadcasted_iota(jnp.int32, (SPAN, SPAN), 0)
    t = lax.broadcasted_iota(jnp.int32, (SPAN, SPAN), 1)
    upto = jnp.where(s <= t, 1.0, 0.0).astype(F32)
    return nn(-rate * dt, upto, HIGHEST)


def two_rows(ref, k):
    top = jnp.broadcast_to(ref[pl.ds(2 * k, 1), :], (WIDTH, ref.shape[1]))
    low = jnp.broadcast_to(ref[pl.ds(2 * k + 1, 1), :], (WIDTH, ref.shape[1]))
    return jnp.concatenate([top, low], axis=0)


def split(v):
    high = v.astype(BF16)
    return high, (v - high.astype(F32)).astype(BF16)


PARTS = ((0, 384, "xyz"), (384, 384, "yzx"), (768, 256, "zxy"))
HALF = SPAN // 2


def tile(v):
    return v.reshape(8, 8, STATE)


def mixer_kernel(
    x_hbm, k_hbm, q_hbm, dt_hbm, dl_hbm, sk_hbm, w_hbm, og_hbm,
    gv_hbm, gk_ref, gq_ref, gs_ref, smo_ref, gw_ref,
    x_ref, k_ref, q_ref, dt_ref, dl_ref, sk_ref, w_ref, og_ref,
    run2, crow, wrow, erow, skrow, frow, rrow, urow, xrow, vrow,
    gbuf, xt_ref, gt_ref, t_ref, e_ref, d_ref, tp, ep, dp,
    upf, gotf, backf, homef, upb, gotb, backb, homeb,
    s_ref, ds_ref, give_s, give_d,
    scores, acc, qacc, kacc, ysum, yp, dxt, gv_ref,
    f_og, r_og, f_q, r_q, r_e, rhs, dw,
    a0, a1, a2, b0, b1, b2, ra0, ra1, ra2, rb0, rb1, rb2, rc0, rc1, rc2,
    s_core, s_x, s_y, s_z,
    in_sem, out_sem, core_send, core_recv, plane_send, plane_recv,
    first_send, first_recv, send, recv,
):
    y, me = lax.axis_index("rec"), lax.axis_index("tm")
    c, g = lax.rem(me, 2), lax.div(me, 2)
    x, z = lax.div(g, 4), lax.rem(g, 4)
    partner = me + 1 - 2 * c
    coord = {"x": x, "y": y, "z": z}
    own = c == 0

    loads = [
        pltpu.make_async_copy(src, dst, in_sem.at[n])
        for n, (src, dst) in enumerate((
            (dt_hbm, dt_ref), (dl_hbm, dl_ref), (x_hbm, x_ref), (k_hbm, k_ref),
            (q_hbm, q_ref), (og_hbm, og_ref), (w_hbm, w_ref), (sk_hbm, sk_ref),
        ))
    ]
    for n in loads:
        n.start()

    def device(axis, value):
        if axis == "x":
            return (y, (value * 4 + z) * 2 + c)
        if axis == "z":
            return (y, (x * 4 + value) * 2 + c)
        return (value, me)

    def other(axis, d):
        return lax.rem(coord[axis] + d, 4)

    def peer(d):
        return lax.rem(g + d, CHIPS)

    barrier = pltpu.get_barrier_semaphore()
    pl.semaphore_signal(barrier, inc=1, device_id=(y, partner), device_id_type=MESH)
    for d in range(1, CHIPS):
        pl.semaphore_signal(barrier, inc=1, device_id=(y, peer(d) * 2 + c), device_id_type=MESH)
    for d in range(1, 4):
        pl.semaphore_signal(barrier, inc=1, device_id=device("y", other("y", d)), device_id_type=MESH)

    def core_copy(src, dst, n):
        return pltpu.make_async_remote_copy(
            src_ref=src, dst_ref=dst, send_sem=core_send.at[n], recv_sem=core_recv.at[n],
            device_id=(y, partner), device_id_type=MESH,
        )

    def both(a, b):
        return jnp.where(own, a, b), jnp.where(own, b, a)

    loads[0].wait()
    loads[1].wait()
    dt = dt_ref[...]
    rate = jnp.exp(column(dl_ref[...]))
    run = running_sums(dt, rate)
    end = run[:, SPAN - 1 :]
    wrow[...] = jnp.exp(end - run) * dt
    erow[...] = jnp.exp(run)
    run2[...] = run * LOG2E
    crow[...] = run * LOG2E - jnp.log2(dt)
    vrow[...] = jnp.broadcast_to(jnp.exp(end), (HEADS, STATE))
    for h in range(HEADS):
        d_ref[h // 2, h % 2] = jnp.broadcast_to(vrow[h : h + 1, :], (8, STATE))

    loads[2].wait()
    loads[3].wait()

    def local_state(i, carry):
        at = pl.ds(pl.multiple_of(i * PAIR, PAIR), PAIR)
        xt = x_ref[:, at].T
        xt_ref[at, :] = xt
        high, low = split(xt.astype(F32) * two_rows(wrow, i))
        t_ref[i] = (nn(high, k_ref[...]) + nn(low, k_ref[...])).reshape(2, 8, 8, STATE)
        return carry

    lax.fori_loop(0, CHIPS, local_state, 0)
    pl.semaphore_wait(barrier, CHIPS + 3)
    swaps = [core_copy(d_ref, dp, 0), core_copy(t_ref.at[:, 1 - c], tp, 2)]
    for n in swaps:
        n.start()
    for n in loads[4:]:
        n.wait()
    for n in swaps:
        n.wait()

    def combine_forward(i, carry):
        d0, d1 = both(d_ref[i, c], dp[i, c])
        t0, t1 = both(t_ref[i, c], tp[i])
        upf[i, 0:8] = d1[None] * t0 + t1
        upf[i, 8] = d0 * d1
        return carry

    lax.fori_loop(0, CHIPS, combine_forward, 0)

    def spread(src, dst, n):
        return [
            pltpu.make_async_remote_copy(
                src_ref=src.at[peer(d)], dst_ref=dst.at[g],
                send_sem=plane_send.at[n, d], recv_sem=plane_recv.at[n, d],
                device_id=(y, peer(d) * 2 + c), device_id_type=MESH,
            )
            for d in range(1, CHIPS)
        ]

    def start(copies):
        for n in copies:
            n.start()
        return copies

    def wait(copies):
        for n in copies:
            n.wait()

    forward_out = start(spread(upf, gotf, 0))
    gotf[g] = upf[g]

    f_og[...] = og_ref[...].astype(F32)
    f_q[...] = q_ref[...].astype(F32)
    early = start([core_copy(f_og, r_og, 3), core_copy(f_q, r_q, 4), core_copy(erow, r_e, 5)])

    def cotangent(m, carry):
        rows = pl.ds(pl.multiple_of(m * 512, 512), 512)
        gbuf[...] = nt(w_ref[rows, :], og_ref[...])
        for n in range(4):
            i = m * 4 + n
            at = pl.ds(pl.multiple_of(i * PAIR, PAIR), PAIR)
            gm = gbuf[n * PAIR : (n + 1) * PAIR, :]
            gt_ref[at, :] = gm
            high, low = split(gm * two_rows(erow, i))
            e_ref[i] = (nn(high, q_ref[...]) + nn(low, q_ref[...])).reshape(2, 8, 8, STATE)
        return carry

    lax.fori_loop(0, 4, cotangent, 0)
    swap_e = start([core_copy(e_ref.at[:, 1 - c], ep, 6)])
    wait(swap_e)

    def combine_backward(i, carry):
        d0, d1 = both(d_ref[i, c], dp[i, c])
        e0, e1 = both(e_ref[i, c], ep[i])
        upb[i, 0:8] = e0 + d0[None] * e1
        upb[i, 8] = d0 * d1
        return carry

    lax.fori_loop(0, CHIPS, combine_backward, 0)
    wait(forward_out)
    carried = jnp.zeros((8, 8, STATE), F32)
    for i in range(CHIPS):
        backf[i] = carried
        carried = gotf[i, 8][None] * carried + gotf[i, 0:8]
    forward_in = start(spread(backf, homef, 1))
    homef[g] = backf[g]
    backward_out = start(spread(upb, gotb, 2))
    gotb[g] = upb[g]

    skrow[...] = jnp.broadcast_to(column(sk_ref[...]), (HEADS, SPAN))
    jj = lax.broadcasted_iota(jnp.int32, (SPAN, SPAN), 0)
    ii = lax.broadcasted_iota(jnp.int32, (SPAN, SPAN), 1)
    causal = jj <= ii
    scores[...] = jnp.where(causal, nt(k_ref[...], q_ref[...]), 0.0)
    acc[...] = jnp.zeros_like(acc)
    qacc[...] = jnp.zeros_like(qacc)
    kacc[...] = jnp.zeros_like(kacc)

    def row_sums(ref, value, i):
        for e in range(2):
            ref[pl.ds(2 * i + e, 1), :] = jnp.sum(
                value[e * WIDTH : (e + 1) * WIDTH], axis=0, keepdims=True
            )

    def inside(i, carry):
        at = pl.ds(pl.multiple_of(i * PAIR, PAIR), PAIR)
        xp = x_ref[:, at]
        xt = xt_ref[at, :]
        gf = gt_ref[at, :]
        gh, gl = split(gf)
        x2 = jnp.concatenate([xp, xp], axis=1)
        y_parts, yl_parts, dx_parts = [], [], []
        for e in range(2):
            row = run2[pl.ds(2 * i + e, 1), :]
            ccol = jnp.broadcast_to(crow[pl.ds(2 * i + e, 1), :], (HALF, SPAN)).T
            d00 = jnp.exp2(jnp.minimum(row[:, :HALF] - ccol[:HALF], 2.0))
            d01 = jnp.exp2(row[:, HALF:] - ccol[:HALF])
            d11 = jnp.exp2(jnp.minimum(row[:, HALF:] - ccol[HALF:], 2.0))
            n00, l00 = split(d00 * scores[:HALF, :HALF])
            n01, l01 = split(d01 * scores[:HALF, HALF:])
            n11, l11 = split(d11 * scores[HALF:, HALF:])
            n10 = jnp.zeros((HALF, HALF), BF16)

            def square(a, b, d):
                top = jnp.concatenate([a, b], axis=1)
                return jnp.concatenate([top, jnp.concatenate([n10, d], axis=1)], axis=0)

            n = square(n00, n01, n11)
            part = slice(e * WIDTH, (e + 1) * WIDTH)
            y_parts.append(nn(xt[part], n))
            yl_parts.append(nn(xt[part], square(l00, l01, l11)))
            dx = nt(jnp.concatenate([gh[part], gl[part]], axis=0), n)
            dx_parts.append(dx[:WIDTH] + dx[WIDTH:])
            blank = jnp.zeros((WIDTH, SPAN), BF16)
            if e == 0:
                gz = jnp.concatenate([gh[part], blank, gl[part], blank], axis=0)
            else:
                gz = jnp.concatenate([blank, gh[part], blank, gl[part]], axis=0)
            dn = nn(x2, gz)
            acc[:HALF, :HALF] += dn[:HALF, :HALF] * d00
            acc[:HALF, HALF:] += dn[:HALF, HALF:] * d01
            acc[HALF:, HALF:] += dn[HALF:, HALF:] * d11
        xf = xt.astype(F32)
        yy = jnp.concatenate(y_parts, axis=0)
        dx = jnp.concatenate(dx_parts, axis=0)
        whole = yy + jnp.concatenate(yl_parts, axis=0) + two_rows(skrow, i) * xf
        ysum[i] = whole.reshape(2, WIDTH, SPAN)
        dxt[at, :] = dx
        row_sums(frow, gf * yy, i)
        row_sums(rrow, xf * dx, i)
        row_sums(xrow, gf * xf, i)
        return carry

    lax.fori_loop(0, CHIPS // 2, inside, 0)
    wait(backward_out)
    carried = jnp.zeros((8, 8, STATE), F32)
    for i in range(CHIPS - 1, -1, -1):
        backb[i] = carried
        carried = gotb[i, 8][None] * carried + gotb[i, 0:8]
    backward_in = start(spread(backb, homeb, 3))
    homeb[g] = backb[g]
    lax.fori_loop(CHIPS // 2, CHIPS, inside, 0)
    wait(early)
    swap_y = start([core_copy(ysum.at[:, 1 - c], yp, 7)])
    rhs[:SPAN] = og_ref[...]
    rhs[SPAN:] = r_og[...].astype(BF16)
    s_mine, s_other = q_ref[...], r_q[...].astype(BF16)
    wait(swap_y)
    wait(forward_in)

    recv_a, recv_b, recv_c = (ra0, ra1, ra2), (rb0, rb1, rb2), (rc0, rc1, rc2)
    first = ([], [], [])

    def first_copy(p, axis, d, src, dst, n):
        return pltpu.make_async_remote_copy(
            src_ref=src, dst_ref=dst, send_sem=first_send.at[n], recv_sem=first_recv.at[n],
            device_id=device(axis, other(axis, d)), device_id_type=MESH,
        )

    def across(states, queries):
        high, low = split(states)
        return nt(high, queries) + nt(low, queries)

    for step, turn in enumerate((2, 1, 3, 0)):
        m = other("x", turn)
        own_states, other_states, own_rows, other_rows, own_y, other_y = [], [], [], [], [], []
        for n in range(4):
            i = m * 4 + n
            d0, _ = both(d_ref[i, c], dp[i, c])
            t0, _ = both(t_ref[i, c], tp[i])
            s0 = homef[i]
            s1 = d0[None] * s0 + t0
            mine, theirs = both(s0, s1)
            s_ref[i, c] = mine
            give_s[i] = theirs
            own_states.append(mine.reshape(WIDTH, STATE))
            other_states.append(theirs.reshape(WIDTH, STATE))
            own_rows.append(jnp.broadcast_to(erow[pl.ds(2 * i + c, 1), :], (WIDTH, SPAN)))
            other_rows.append(jnp.broadcast_to(r_e[pl.ds(2 * i + c, 1), :], (WIDTH, SPAN)))
            own_y.append(ysum[i, c])
            other_y.append(yp[i])

        def join(parts):
            return jnp.concatenate(parts, axis=0)

        left = join(own_y) + across(join(own_states), s_mine) * join(own_rows)
        right = join(other_y) + across(join(other_states), s_other) * join(other_rows)
        lhs = jnp.concatenate([left.astype(BF16), right.astype(BF16)], axis=1)
        dw[m] = nn(lhs, rhs[...]).reshape(4, 4, 16, MODEL)
        copies = []
        if turn:
            at = (slice(None), slice(None), slice(None), pl.ds(PARTS[0][0], PARTS[0][1]))
            cp = first_copy(0, "x", turn, dw.at[(m,) + at], ra0.at[turn - 1], turn - 1)
            first[0].append(cp)
            copies.append(cp)
        for d in range(1, 4):
            cols = (slice(None), pl.ds(PARTS[1][0], PARTS[1][1]))
            src = dw.at[(m, slice(None), other("y", d)) + cols]
            cp = first_copy(1, "y", d, src, ra1.at[d - 1, m], 3 + step * 3 + d - 1)
            first[1].append(cp)
            copies.append(cp)
            cols = (slice(None), pl.ds(PARTS[2][0], PARTS[2][1]))
            src = dw.at[(m, other("z", d), slice(None)) + cols]
            cp = first_copy(2, "z", d, src, ra2.at[d - 1, m], 15 + step * 3 + d - 1)
            first[2].append(cp)
            copies.append(cp)
        start(copies)

    swap_s = start([core_copy(give_s, s_ref.at[:, c], 8)])
    wait(backward_in)

    def finish_backward(i, carry):
        d0, d1 = both(d_ref[i, c], dp[i, c])
        e0, e1 = both(e_ref[i, c], ep[i])
        b1 = homeb[i]
        b0 = d1[None] * b1 + e1
        ds_ref[i, c], give_d[i] = both(b0, b1)
        return carry

    lax.fori_loop(0, CHIPS, finish_backward, 0)
    swap_d = start([core_copy(give_d, ds_ref.at[:, c], 9)])
    wait(swap_s)
    wait(swap_d)

    def outside(i, carry):
        at = pl.ds(pl.multiple_of(i * PAIR, PAIR), PAIR)
        xf = xt_ref[at, :].astype(F32)
        gf = gt_ref[at, :]
        wp = two_rows(wrow, i)
        ep2 = two_rows(erow, i)
        sp = s_ref[i].reshape(PAIR, STATE)
        dsp = ds_ref[i].reshape(PAIR, STATE)
        sh, sl = split(sp)
        dsh, dsl = split(dsp)
        yy = (nt(sh, q_ref[...]) + nt(sl, q_ref[...])) * ep2
        dxs = (nt(dsh, k_ref[...]) + nt(dsl, k_ref[...])) * wp
        gv_ref[:, at] = (dxt[at, :] + dxs + two_rows(skrow, i) * gf).T
        ge = (gf * ep2).astype(BF16)
        xw = (xf * wp).astype(BF16)
        qacc[...] += nn(sh.T, ge) + nn(sl.T, ge)
        kacc[...] += nn(dsh.T, xw) + nn(dsl.T, xw)
        fg, xd, sd = gf * yy, xf * dxs, sp * dsp
        for e in range(2):
            part = slice(e * WIDTH, (e + 1) * WIDTH)
            h = pl.ds(2 * i + e, 1)
            frow[h, :] += jnp.sum(fg[part], axis=0, keepdims=True)
            urow[h, :] = jnp.sum(xd[part], axis=0, keepdims=True)
            vrow[h, :] = jnp.sum(sd[part], axis=0, keepdims=True)
        return carry

    lax.fori_loop(0, CHIPS, outside, 0)
    store = pltpu.make_async_copy(gv_ref, gv_hbm, out_sem)
    store.start()
    dst = jnp.where(causal, acc[...], 0.0).astype(BF16)
    gk_ref[...] = nn(dst, q_ref[...]) + kacc[...].T
    gq_ref[...] = (nn(k_ref[...].T, dst) + qacc[...]).T
    upto = jnp.where(ii <= jj, 1.0, 0.0).astype(F32)
    decay = jnp.exp(run2[:, SPAN - 1 :] * (1.0 / LOG2E))
    dt = dt_ref[...]
    rate = jnp.exp(column(dl_ref[...]))
    tail = jnp.sum(urow[...], axis=1, keepdims=True)
    tail = tail + decay * jnp.sum(vrow[...], axis=1, keepdims=True)
    r = rrow[...] + urow[...]
    da = nn(frow[...] - r, upto, HIGHEST) + tail
    gs_ref[...] = r / dt - rate * da
    g_decay = jnp.sum(-rate * dt * da, axis=1, keepdims=True)
    g_skip = jnp.sum(xrow[...], axis=1, keepdims=True)
    lane = lax.broadcasted_iota(jnp.int32, (HEADS, 128), 1)
    s_core[c] = jnp.where(lane == 0, g_decay, jnp.where(lane == 1, g_skip, 0.0))
    wait(start([core_copy(s_core.at[c], s_core.at[c], 10)]))

    def reach(axis, d, src, dst, n):
        return pltpu.make_async_remote_copy(
            src_ref=src, dst_ref=dst, send_sem=send.at[n, d - 1], recv_sem=recv.at[n, d - 1],
            device_id=device(axis, other(axis, d)), device_id_type=MESH,
        )

    def small_start(axis, buf, value, n):
        buf[coord[axis]] = value
        mine = buf.at[coord[axis]]
        return start([reach(axis, d, mine, mine, n) for d in range(1, 4)])

    def small_sum(copies, buf):
        wait(copies)
        return (buf[0] + buf[1]) + (buf[2] + buf[3])

    def pick(dims, axis, value):
        return tuple(value if n == axis else slice(None) for n in dims)

    def reduce_start(src, dims, axis, dst, n):
        return start([
            reach(axis, d, src.at[pick(dims, axis, other(axis, d))], dst.at[d - 1], n) for d in range(1, 4)
        ])

    sums_a, sums_b = (a0, a1, a2), (b0, b1, b2)
    dims = "xzy"
    small = small_start("x", s_x, s_core[0] + s_core[1], 9)
    second, third, last = [], [], []
    for p, (low, wide, order) in enumerate(PARTS):
        wait(first[p])
        at = pick(dims, order[0], coord[order[0]]) + (slice(None), pl.ds(low, wide))
        got = recv_a[p]
        sums_a[p][...] = (dw[at] + got[0]) + (got[1] + got[2])
        rest = dims.replace(order[0], "")
        second.append(reduce_start(sums_a[p], rest, order[1], recv_b[p], p))
    small = small_start("y", s_y, small_sum(small, s_x), 10)
    for p, (low, wide, order) in enumerate(PARTS):
        wait(second[p])
        rest = dims.replace(order[0], "")
        at = pick(rest, order[1], coord[order[1]])
        got = recv_b[p]
        sums_b[p][...] = (sums_a[p][at] + got[0]) + (got[1] + got[2])
        third.append(reduce_start(sums_b[p], order[2], order[2], recv_c[p], 3 + p))
    small = small_start("z", s_z, small_sum(small, s_y), 11)
    rows = pl.ds(pl.multiple_of(y * 16, 16), 16)
    for p, (low, wide, order) in enumerate(PARTS):
        wait(third[p])
        got = recv_c[p]
        cols = pl.ds(low, wide)
        gw_ref[rows, cols] = (sums_b[p][coord[order[2]]] + got[0]) + (got[1] + got[2])
        mine = gw_ref.at[rows, cols]
        last.extend(start([reach("y", d, mine, mine, 6 + p) for d in range(1, 4)]))
    smo_ref[...] = small_sum(small, s_z)
    store.wait()
    wait(last)


def sds(shape, dtype=F32):
    return jax.ShapeDtypeStruct(shape, dtype)


def local(token_values, write_keys, read_queries, step_sizes, decay_log, skip_gain, out_weight, out_grad):
    x, k, q, dt, og = token_values[0], write_keys[0], read_queries[0], step_sizes[0], out_grad[0]
    dl, sk = decay_log.reshape(1, HEADS), skip_gain.reshape(1, HEADS)
    vm, dma = pltpu.VMEM, pltpu.SemaphoreType.DMA
    anywhere = pl.BlockSpec(memory_space=pl.ANY)
    inside = pl.BlockSpec(memory_space=pltpu.VMEM)
    row = vm((HEADS, SPAN), F32)
    heads = vm((CHIPS, 8, 8, STATE), F32)
    packed = vm((CHIPS, 9, 8, STATE), F32)
    pairs = vm((CHIPS, 2, 8, 8, STATE), F32)
    wides = [w for _, w, _ in PARTS]
    gv, gk, gq, gs, small, gw = pl.pallas_call(
        mixer_kernel,
        out_shape=(
            sds((SPAN, INNER)), sds((SPAN, STATE)), sds((SPAN, STATE)), sds((HEADS, SPAN)),
            sds((HEADS, 128)), sds((64, MODEL)),
        ),
        in_specs=[anywhere] * 8,
        out_specs=(anywhere,) + (inside,) * 5,
        scratch_shapes=[
            vm((SPAN, INNER), BF16), vm((SPAN, STATE), BF16), vm((SPAN, STATE), BF16), row,
            vm((1, HEADS), F32), vm((1, HEADS), F32), vm((INNER, MODEL), BF16), vm((SPAN, MODEL), BF16),
            row, row, row, row, row, row, row, row, row, vm((HEADS, STATE), F32),
            vm((512, SPAN), F32), vm((INNER, SPAN), BF16), vm((INNER, SPAN), F32),
            pairs, pairs, vm((CHIPS, 2, 8, STATE), F32), heads, heads, vm((CHIPS, 2, 8, STATE), F32),
            packed, packed, heads, heads, packed, packed, heads, heads,
            pairs, pairs, heads, heads,
            vm((SPAN, SPAN), F32), vm((SPAN, SPAN), F32), vm((STATE, SPAN), F32), vm((STATE, SPAN), F32),
            vm((CHIPS, 2, WIDTH, SPAN), F32), vm((CHIPS, WIDTH, SPAN), F32),
            vm((INNER, SPAN), F32), vm((SPAN, INNER), F32),
            vm((SPAN, MODEL), F32), vm((SPAN, MODEL), F32), vm((SPAN, STATE), F32), vm((SPAN, STATE), F32),
            row, vm((2 * SPAN, MODEL), BF16), vm((4, 4, 4, 16, MODEL), F32),
            *[vm((4, 4, 16, w), F32) for w in wides],
            *[vm((4, 16, w), F32) for w in wides],
            *[vm((3, 4, 4, 16, w), F32) for w in wides],
            *[vm((3, 4, 16, w), F32) for w in wides],
            *[vm((3, 16, w), F32) for w in wides],
            vm((2, HEADS, 128), F32),
            *[vm((4, HEADS, 128), F32)] * 3,
            dma((8,)), dma, dma((11,)), dma((11,)), dma((4, CHIPS)), dma((4, CHIPS)),
            dma((27,)), dma((27,)), dma((12, 3)), dma((12, 3)),
        ],
        compiler_params=pltpu.CompilerParams(
            vmem_limit_bytes=60 * 1024 * 1024, collective_id=0, has_side_effects=True
        ),
        name="mixer",
    )(x, k, q, dt, dl, sk, out_weight, og)
    return gv[None], gk[None], gq[None], gs[None], small[:, 0], small[:, 1], gw


def solution(mesh):
    by_time = P("rec", "tm", None)
    by_head = P("rec", None, "tm")
    return jax.shard_map(
        local,
        mesh=mesh,
        in_specs=(by_time, by_time, by_time, by_head, P(), P(), P(), by_time),
        out_specs=(by_time, by_time, by_time, by_head, P(), P(), P("tm", None)),
        check_vma=False,
    )
```

time: 504 us -> 90.3 us (0.18)
  waiting for transfers between devices: 135 us -> 0 us
  other arithmetic: 112 us -> 0 us
  blocking collectives: 88 us -> 0 us
  Pallas kernels: 0 us -> 82 us
  local copies, waits for them, and re-layouts: 82.2 us -> 7.33 us
  matrix products: 66.7 us -> 0 us
  between operations: 14.2 us -> 0.65 us
    all_gather x2 -> x0, waiting for transfers between devices: 135 us -> none  [prefix(): pieces = jax.tree.map(lambda part: lax.all_gather(part, axis), value)]
    select_n x62 -> x0, other arithmetic: 91.5 us -> none  [hop(): jnp.where(position < mine, new, old)]
    pallas_call x0 -> x1, Pallas kernels: none -> 82 us  [local(): pl.pallas_call(mixer_kernel, out_shape=(sds((SPAN, INNER)), sds((SPAN, ST...]
    dot_general x14 -> x0, matrix products: 66.7 us -> none  [the longest x3 35.7 us: block_terms(): jnp.einsum('hij,jhp->ihp', decay_mat * scores[None], scaled, precision=la...]
    psum x1 -> x0, blocking collectives: 64.9 us -> none  [local(): grad_decay, grad_skip = lax.psum((decay_part, skip_part), ('rec', 'tm'))]
    mul x77 -> x0, local copies, waits for them, and re-layouts: 44.9 us -> none  [the longest x62 20.1 us: chain(): late_decay[:, :, None, None] * early_state + late_state]
    rev x2 -> x0, local copies, waits for them, and re-layouts: 24.3 us -> none  [prefix(): pieces = jax.tree.map(lambda part: part[::-1], pieces)]
    all_gather x1 -> x0, blocking collectives: 23 us -> none  [prefix(): pieces = jax.tree.map(lambda part: lax.all_gather(part, axis), value)]
  transfers between devices with their start and end apart: 4 -> 0, of which waited for: 2 -> 0; matrix products, arithmetic and copies ran while one was open for 37% -> 0% of each run, Pallas kernels for 0% -> 0%
where the time goes in v2:
time: 90.3 us; the launch traced here: 90 us
  Pallas kernels  82 us (91%)
  local copies, waits for them, and re-layouts  7.33 us (8%)
    pallas_call x1, Pallas kernels, local(): pl.pallas_call(mixer_kernel, out_shape=(sds((SPAN, INNER)), sds((SPAN, ST...  82 us
    unnamed x13, local copies, waits for them, and re-layouts  5.84 us

profile of v2, /device:TPU:0, one launch (start us, length us, event | category | flops | bytes accessed | tf_op | source)
XLA Modules:
  0.0 90.0 jit_solution(6901475640990840576)
XLA Ops:
  0.6 82.0 %mixer.1 = (f32[256,2048]{1,0:T(8,128)}, f32[256,128]{1,0:T(8,128)}, f32[256,128]{1,0:T(8,128)}, f32[32,256]{1,0:T(8,128)}, f32[32,128]{1,0:T(8,128)}, /*index=5*/f32[64,1024]{1,0:T(8,128)}) custom-call(bf16[256,2048]{1,0:T(8,128)(2,1)} %bitcast.12, bf16[256,128]{1,0:T(8,128)(2,1)} %bitcast.16, bf16[256,128]{1,0:T(8,128)(2,1)} %bitcast.17, ...), custom_call_target="tpu_custom_call" | custom-call | tf_op jit(solution)/shard_map/mixer/pallas_call | solution.py:506
  82.7 1.5 %slice_reduce_fusion = (f32[32]{0:T(128)}, f32[32]{0:T(128)}) fusion(f32[32,128]{1,0:T(8,128)} %get-tuple-element.17), kind=kLoop, calls=%fused_computation | loop fusion | bytes 512 | tf_op jit(solution)/shard_map/slice | solution.py:542
  84.2 0.0 copy-start.2
  84.2 0.0 copy-start.1
  84.2 0.0 copy-start.3
  84.2 0.0 copy-start
  84.2 3.2 %copy.20 = f32[1,256,2048]{2,1,0:T(8,128)} copy(f32[1,256,2048]{2,1,0:T(8,128)} %bitcast.11) | data formatting | bytes 4194304
  87.4 0.0 copy-done.2
  87.4 0.7 copy.21
  88.0 0.0 copy-done.1
  88.0 0.7 copy.22
  88.7 0.0 copy-done.3
  88.7 0.6 copy.23
  89.3 0.0 copy-done
  89.3 0.7 copy.24
Async XLA Ops:
  84.2 3.2 %copy-start.2 = (f32[256,128]{1,0:T(8,128)S(1)}, f32[256,128]{1,0:T(8,128)}, u32[]{:S(2)}) copy-start(f32[256,128]{1,0:T(8,128)} %get-tuple-element.14) | copy-start | bytes 393220
  84.2 3.9 %copy-start.1 = (f32[256,128]{1,0:T(8,128)S(1)}, f32[256,128]{1,0:T(8,128)}, u32[]{:S(2)}) copy-start(f32[256,128]{1,0:T(8,128)} %get-tuple-element.15) | copy-start | bytes 393220
  84.2 4.5 %copy-start.3 = (f32[32,256]{1,0:T(8,128)S(1)}, f32[32,256]{1,0:T(8,128)}, u32[]{:S(2)}) copy-start(f32[32,256]{1,0:T(8,128)} %get-tuple-element.16) | copy-start | bytes 98308
  84.2 5.1 %copy-start = (f32[64,1024]{1,0:T(8,128)S(1)}, f32[64,1024]{1,0:T(8,128)}, u32[]{:S(2)}) copy-start(f32[64,1024]{1,0:T(8,128)} %get-tuple-element.34) | copy-start | bytes 786436

commit v3 on v2

--- a/solution.py
+++ b/solution.py
@@ -57,7 +57,7 @@
     return high, (v - high.astype(F32)).astype(BF16)
 
 
-PARTS = ((0, 384, "xyz"), (384, 384, "yzx"), (768, 256, "zxy"))
+PARTS = ((640, "xyz"), (768, "yzx"), (640, "zxy"))
 HALF = SPAN // 2
 
 
@@ -74,8 +74,8 @@
     upf, gotf, backf, homef, upb, gotb, backb, homeb,
     s_ref, ds_ref, give_s, give_d,
     scores, acc, qacc, kacc, ysum, yp, dxt, gv_ref,
-    f_og, r_og, f_q, r_q, r_e, rhs, dw,
-    a0, a1, a2, b0, b1, b2, ra0, ra1, ra2, rb0, rb1, rb2, rc0, rc1, rc2,
+    f_og, r_og, f_q, r_q, r_e, rhs, dw0, dw1, dw2,
+    a0, a1, a2, b0, b1, b2, ra0, ra1, ra2, rb0, rb1, rb2, rc0, rc1, rc2, w0, w1, w2,
     s_core, s_x, s_y, s_z,
     in_sem, out_sem, core_send, core_recv, plane_send, plane_recv,
     first_send, first_recv, send, recv,
@@ -125,6 +125,25 @@
 
     def both(a, b):
         return jnp.where(own, a, b), jnp.where(own, b, a)
+
+    def start(copies):
+        for n in copies:
+            n.start()
+        return copies
+
+    def wait(copies):
+        for n in copies:
+            n.wait()
+
+    def spread(src, dst, n):
+        return [
+            pltpu.make_async_remote_copy(
+                src_ref=src.at[peer(d)], dst_ref=dst.at[g],
+                send_sem=plane_send.at[n, d], recv_sem=plane_recv.at[n, d],
+                device_id=(y, peer(d) * 2 + c), device_id_type=MESH,
+            )
+            for d in range(1, CHIPS)
+        ]
 
     loads[0].wait()
     loads[1].wait()
@@ -152,50 +171,6 @@
         return carry
 
     lax.fori_loop(0, CHIPS, local_state, 0)
-    pl.semaphore_wait(barrier, CHIPS + 3)
-    swaps = [core_copy(d_ref, dp, 0), core_copy(t_ref.at[:, 1 - c], tp, 2)]
-    for n in swaps:
-        n.start()
-    for n in loads[4:]:
-        n.wait()
-    for n in swaps:
-        n.wait()
-
-    def combine_forward(i, carry):
-        d0, d1 = both(d_ref[i, c], dp[i, c])
-        t0, t1 = both(t_ref[i, c], tp[i])
-        upf[i, 0:8] = d1[None] * t0 + t1
-        upf[i, 8] = d0 * d1
-        return carry
-
-    lax.fori_loop(0, CHIPS, combine_forward, 0)
-
-    def spread(src, dst, n):
-        return [
-            pltpu.make_async_remote_copy(
-                src_ref=src.at[peer(d)], dst_ref=dst.at[g],
-                send_sem=plane_send.at[n, d], recv_sem=plane_recv.at[n, d],
-                device_id=(y, peer(d) * 2 + c), device_id_type=MESH,
-            )
-            for d in range(1, CHIPS)
-        ]
-
-    def start(copies):
-        for n in copies:
-            n.start()
-        return copies
-
-    def wait(copies):
-        for n in copies:
-            n.wait()
-
-    forward_out = start(spread(upf, gotf, 0))
-    gotf[g] = upf[g]
-
-    f_og[...] = og_ref[...].astype(F32)
-    f_q[...] = q_ref[...].astype(F32)
-    early = start([core_copy(f_og, r_og, 3), core_copy(f_q, r_q, 4), core_copy(erow, r_e, 5)])
-
     def cotangent(m, carry):
         rows = pl.ds(pl.multiple_of(m * 512, 512), 512)
         gbuf[...] = nt(w_ref[rows, :], og_ref[...])
@@ -208,9 +183,27 @@
             e_ref[i] = (nn(high, q_ref[...]) + nn(low, q_ref[...])).reshape(2, 8, 8, STATE)
         return carry
 
+    wait(loads[4:])
     lax.fori_loop(0, 4, cotangent, 0)
-    swap_e = start([core_copy(e_ref.at[:, 1 - c], ep, 6)])
-    wait(swap_e)
+    pl.semaphore_wait(barrier, CHIPS + 3)
+    swaps = start([
+        core_copy(d_ref, dp, 0), core_copy(t_ref.at[:, 1 - c], tp, 1), core_copy(e_ref.at[:, 1 - c], ep, 2)
+    ])
+    wait(swaps[:2])
+
+    def combine_forward(i, carry):
+        d0, d1 = both(d_ref[i, c], dp[i, c])
+        t0, t1 = both(t_ref[i, c], tp[i])
+        upf[i, 0:8] = d1[None] * t0 + t1
+        upf[i, 8] = d0 * d1
+        return carry
+
+    lax.fori_loop(0, CHIPS, combine_forward, 0)
+
+    forward_out = start(spread(upf, gotf, 0))
+    gotf[g] = upf[g]
+
+    wait(swaps[2:])
 
     def combine_backward(i, carry):
         d0, d1 = both(d_ref[i, c], dp[i, c])
@@ -220,15 +213,12 @@
         return carry
 
     lax.fori_loop(0, CHIPS, combine_backward, 0)
-    wait(forward_out)
-    carried = jnp.zeros((8, 8, STATE), F32)
-    for i in range(CHIPS):
-        backf[i] = carried
-        carried = gotf[i, 8][None] * carried + gotf[i, 0:8]
-    forward_in = start(spread(backf, homef, 1))
-    homef[g] = backf[g]
     backward_out = start(spread(upb, gotb, 2))
     gotb[g] = upb[g]
+
+    f_og[...] = og_ref[...].astype(F32)
+    f_q[...] = q_ref[...].astype(F32)
+    early = start([core_copy(f_og, r_og, 3), core_copy(f_q, r_q, 4), core_copy(erow, r_e, 5)])
 
     skrow[...] = jnp.broadcast_to(column(sk_ref[...]), (HEADS, SPAN))
     jj = lax.broadcasted_iota(jnp.int32, (SPAN, SPAN), 0)
@@ -294,7 +284,15 @@
         row_sums(xrow, gf * xf, i)
         return carry
 
-    lax.fori_loop(0, CHIPS // 2, inside, 0)
+    lax.fori_loop(0, 6, inside, 0)
+    wait(forward_out)
+    carried = jnp.zeros((8, 8, STATE), F32)
+    for i in range(CHIPS):
+        backf[i] = carried
+        carried = gotf[i, 8][None] * carried + gotf[i, 0:8]
+    forward_in = start(spread(backf, homef, 1))
+    homef[g] = backf[g]
+    lax.fori_loop(6, 11, inside, 0)
     wait(backward_out)
     carried = jnp.zeros((8, 8, STATE), F32)
     for i in range(CHIPS - 1, -1, -1):
@@ -302,9 +300,9 @@
         carried = gotb[i, 8][None] * carried + gotb[i, 0:8]
     backward_in = start(spread(backb, homeb, 3))
     homeb[g] = backb[g]
-    lax.fori_loop(CHIPS // 2, CHIPS, inside, 0)
+    lax.fori_loop(11, CHIPS, inside, 0)
     wait(early)
-    swap_y = start([core_copy(ysum.at[:, 1 - c], yp, 7)])
+    swap_y = start([core_copy(ysum.at[:, 1 - c], yp, 6)])
     rhs[:SPAN] = og_ref[...]
     rhs[SPAN:] = r_og[...].astype(BF16)
     s_mine, s_other = q_ref[...], r_q[...].astype(BF16)
@@ -314,7 +312,7 @@
     recv_a, recv_b, recv_c = (ra0, ra1, ra2), (rb0, rb1, rb2), (rc0, rc1, rc2)
     first = ([], [], [])
 
-    def first_copy(p, axis, d, src, dst, n):
+    def first_copy(axis, d, src, dst, n):
         return pltpu.make_async_remote_copy(
             src_ref=src, dst_ref=dst, send_sem=first_send.at[n], recv_sem=first_recv.at[n],
             device_id=device(axis, other(axis, d)), device_id_type=MESH,
@@ -349,27 +347,27 @@
         left = join(own_y) + across(join(own_states), s_mine) * join(own_rows)
         right = join(other_y) + across(join(other_states), s_other) * join(other_rows)
         lhs = jnp.concatenate([left.astype(BF16), right.astype(BF16)], axis=1)
-        dw[m] = nn(lhs, rhs[...]).reshape(4, 4, 16, MODEL)
+        whole = nn(lhs, rhs[...]).reshape(4, 4, 2, 8, MODEL)
+        dw0[m] = whole[:, :, 0, :, :640]
+        dw2[m] = whole[:, :, 1, :, 384:]
+        for n in range(4):
+            dw1[m, n, :, :, :384] = whole[:, n, 0, :, 640:]
+            dw1[m, n, :, :, 384:] = whole[:, n, 1, :, :384]
         copies = []
         if turn:
-            at = (slice(None), slice(None), slice(None), pl.ds(PARTS[0][0], PARTS[0][1]))
-            cp = first_copy(0, "x", turn, dw.at[(m,) + at], ra0.at[turn - 1], turn - 1)
+            cp = first_copy("x", turn, dw0.at[m], ra0.at[turn - 1], turn - 1)
             first[0].append(cp)
             copies.append(cp)
         for d in range(1, 4):
-            cols = (slice(None), pl.ds(PARTS[1][0], PARTS[1][1]))
-            src = dw.at[(m, slice(None), other("y", d)) + cols]
-            cp = first_copy(1, "y", d, src, ra1.at[d - 1, m], 3 + step * 3 + d - 1)
+            cp = first_copy("y", d, dw1.at[m, other("y", d)], ra1.at[d - 1, m], 3 + step * 3 + d - 1)
             first[1].append(cp)
             copies.append(cp)
-            cols = (slice(None), pl.ds(PARTS[2][0], PARTS[2][1]))
-            src = dw.at[(m, other("z", d), slice(None)) + cols]
-            cp = first_copy(2, "z", d, src, ra2.at[d - 1, m], 15 + step * 3 + d - 1)
+            cp = first_copy("z", d, dw2.at[m, other("z", d)], ra2.at[d - 1, m], 15 + step * 3 + d - 1)
             first[2].append(cp)
             copies.append(cp)
         start(copies)
 
-    swap_s = start([core_copy(give_s, s_ref.at[:, c], 8)])
+    swap_s = start([core_copy(give_s, s_ref.at[:, c], 7)])
     wait(backward_in)
 
     def finish_backward(i, carry):
@@ -381,7 +379,7 @@
         return carry
 
     lax.fori_loop(0, CHIPS, finish_backward, 0)
-    swap_d = start([core_copy(give_d, ds_ref.at[:, c], 9)])
+    swap_d = start([core_copy(give_d, ds_ref.at[:, c], 8)])
     wait(swap_s)
     wait(swap_d)
 
@@ -430,7 +428,7 @@
     g_skip = jnp.sum(xrow[...], axis=1, keepdims=True)
     lane = lax.broadcasted_iota(jnp.int32, (HEADS, 128), 1)
     s_core[c] = jnp.where(lane == 0, g_decay, jnp.where(lane == 1, g_skip, 0.0))
-    wait(start([core_copy(s_core.at[c], s_core.at[c], 10)]))
+    wait(start([core_copy(s_core.at[c], s_core.at[c], 9)]))
 
     def reach(axis, d, src, dst, n):
         return pltpu.make_async_remote_copy(
@@ -455,37 +453,57 @@
             reach(axis, d, src.at[pick(dims, axis, other(axis, d))], dst.at[d - 1], n) for d in range(1, 4)
         ])
 
-    sums_a, sums_b = (a0, a1, a2), (b0, b1, b2)
-    dims = "xzy"
+    parts, sums_a, sums_b, rows = (dw0, dw1, dw2), (a0, a1, a2), (b0, b1, b2), (w0, w1, w2)
+    layouts = ("xzy", "xyz", "xzy")
     small = small_start("x", s_x, s_core[0] + s_core[1], 9)
     second, third, last = [], [], []
-    for p, (low, wide, order) in enumerate(PARTS):
+    for p, (_, order) in enumerate(PARTS):
         wait(first[p])
-        at = pick(dims, order[0], coord[order[0]]) + (slice(None), pl.ds(low, wide))
         got = recv_a[p]
-        sums_a[p][...] = (dw[at] + got[0]) + (got[1] + got[2])
-        rest = dims.replace(order[0], "")
+        mine = parts[p][pick(layouts[p], order[0], coord[order[0]])]
+        sums_a[p][...] = (mine + got[0]) + (got[1] + got[2])
+        rest = layouts[p].replace(order[0], "")
         second.append(reduce_start(sums_a[p], rest, order[1], recv_b[p], p))
     small = small_start("y", s_y, small_sum(small, s_x), 10)
-    for p, (low, wide, order) in enumerate(PARTS):
+    for p, (_, order) in enumerate(PARTS):
         wait(second[p])
-        rest = dims.replace(order[0], "")
-        at = pick(rest, order[1], coord[order[1]])
+        rest = layouts[p].replace(order[0], "")
         got = recv_b[p]
-        sums_b[p][...] = (sums_a[p][at] + got[0]) + (got[1] + got[2])
+        mine = sums_a[p][pick(rest, order[1], coord[order[1]])]
+        sums_b[p][...] = (mine + got[0]) + (got[1] + got[2])
         third.append(reduce_start(sums_b[p], order[2], order[2], recv_c[p], 3 + p))
     small = small_start("z", s_z, small_sum(small, s_y), 11)
-    rows = pl.ds(pl.multiple_of(y * 16, 16), 16)
-    for p, (low, wide, order) in enumerate(PARTS):
+    for p, (_, order) in enumerate(PARTS):
         wait(third[p])
         got = recv_c[p]
-        cols = pl.ds(low, wide)
-        gw_ref[rows, cols] = (sums_b[p][coord[order[2]]] + got[0]) + (got[1] + got[2])
-        mine = gw_ref.at[rows, cols]
-        last.extend(start([reach("y", d, mine, mine, 6 + p) for d in range(1, 4)]))
+        rows[p][y] = (sums_b[p][coord[order[2]]] + got[0]) + (got[1] + got[2])
+        last.extend(start([reach("y", d, rows[p].at[y], rows[p].at[y], 6 + p) for d in range(1, 4)]))
     smo_ref[...] = small_sum(small, s_z)
     store.wait()
     wait(last)
+    for n in range(4):
+        gw_ref[16 * n : 16 * n + 8, :640] = w0[n]
+        gw_ref[16 * n : 16 * n + 8, 640:] = w1[n, :, :384]
+        gw_ref[16 * n + 8 : 16 * n + 16, :384] = w1[n, :, 384:]
+        gw_ref[16 * n + 8 : 16 * n + 16, 384:] = w2[n]
+
+
+def output_kernel(
+    gv, gk, gq, gs, small, gw, gv_out, gk_out, gq_out, gs_out, decay_out, skip_out, gw_out, sem
+):
+    quarter = SPAN // 4
+    pairs = [(gv.at[pl.ds(n * quarter, quarter)], gv_out.at[pl.ds(n * quarter, quarter)]) for n in range(4)]
+    pairs += [(gk, gk_out), (gq, gq_out), (gs, gs_out), (gw, gw_out)]
+    copies = [pltpu.make_async_copy(a, b, sem.at[n]) for n, (a, b) in enumerate(pairs)]
+    for n in copies:
+        n.start()
+    i = lax.broadcasted_iota(jnp.int32, (HEADS, HEADS), 0)
+    j = lax.broadcasted_iota(jnp.int32, (HEADS, HEADS), 1)
+    for n, ref in enumerate((decay_out, skip_out)):
+        whole = jnp.broadcast_to(small[:, n : n + 1], (HEADS, HEADS))
+        ref[...] = jnp.sum(jnp.where(i == j, whole, 0.0), axis=0, keepdims=True)
+    for n in copies:
+        n.wait()
 
 
 def sds(shape, dtype=F32):
@@ -502,8 +520,8 @@
     heads = vm((CHIPS, 8, 8, STATE), F32)
     packed = vm((CHIPS, 9, 8, STATE), F32)
     pairs = vm((CHIPS, 2, 8, 8, STATE), F32)
-    wides = [w for _, w, _ in PARTS]
-    gv, gk, gq, gs, small, gw = pl.pallas_call(
+    wides = [w for w, _ in PARTS]
+    made = pl.pallas_call(
         mixer_kernel,
         out_shape=(
             sds((SPAN, INNER)), sds((SPAN, STATE)), sds((SPAN, STATE)), sds((HEADS, SPAN)),
@@ -523,15 +541,16 @@
             vm((CHIPS, 2, WIDTH, SPAN), F32), vm((CHIPS, WIDTH, SPAN), F32),
             vm((INNER, SPAN), F32), vm((SPAN, INNER), F32),
             vm((SPAN, MODEL), F32), vm((SPAN, MODEL), F32), vm((SPAN, STATE), F32), vm((SPAN, STATE), F32),
-            row, vm((2 * SPAN, MODEL), BF16), vm((4, 4, 4, 16, MODEL), F32),
-            *[vm((4, 4, 16, w), F32) for w in wides],
-            *[vm((4, 16, w), F32) for w in wides],
-            *[vm((3, 4, 4, 16, w), F32) for w in wides],
-            *[vm((3, 4, 16, w), F32) for w in wides],
-            *[vm((3, 16, w), F32) for w in wides],
+            row, vm((2 * SPAN, MODEL), BF16), *[vm((4, 4, 4, 8, w), F32) for w in wides],
+            *[vm((4, 4, 8, w), F32) for w in wides],
+            *[vm((4, 8, w), F32) for w in wides],
+            *[vm((3, 4, 4, 8, w), F32) for w in wides],
+            *[vm((3, 4, 8, w), F32) for w in wides],
+            *[vm((3, 8, w), F32) for w in wides],
+            *[vm((4, 8, w), F32) for w in wides],
             vm((2, HEADS, 128), F32),
             *[vm((4, HEADS, 128), F32)] * 3,
-            dma((8,)), dma, dma((11,)), dma((11,)), dma((4, CHIPS)), dma((4, CHIPS)),
+            dma((8,)), dma, dma((10,)), dma((10,)), dma((4, CHIPS)), dma((4, CHIPS)),
             dma((27,)), dma((27,)), dma((12, 3)), dma((12, 3)),
         ],
         compiler_params=pltpu.CompilerParams(
@@ -539,7 +558,19 @@
         ),
         name="mixer",
     )(x, k, q, dt, dl, sk, out_weight, og)
-    return gv[None], gk[None], gq[None], gs[None], small[:, 0], small[:, 1], gw
+    gv, gk, gq, gs, decay, skip, gw = pl.pallas_call(
+        output_kernel,
+        out_shape=(
+            sds((SPAN, INNER)), sds((SPAN, STATE)), sds((SPAN, STATE)), sds((HEADS, SPAN)),
+            sds((1, HEADS)), sds((1, HEADS)), sds((64, MODEL)),
+        ),
+        in_specs=[anywhere] * 4 + [inside, anywhere],
+        out_specs=(anywhere,) * 4 + (inside,) * 2 + (anywhere,),
+        scratch_shapes=[dma((8,))],
+        compiler_params=pltpu.CompilerParams(vmem_limit_bytes=60 * 1024 * 1024),
+        name="output",
+    )(*made)
+    return gv[None], gk[None], gq[None], gs[None], decay.reshape(HEADS), skip.reshape(HEADS), gw
 
 
 def solution(mesh):

time: 90.3 us -> 164 us (1.82)
  Pallas kernels: 82 us -> 163 us
  local copies, waits for them, and re-layouts: 7.33 us -> 0 us
    pallas_call x0 -> x1, Pallas kernels: none -> 82.8 us  [local(): pl.pallas_call(output_kernel, out_shape=(sds((SPAN, INNER)), sds((SPAN, S...]
    unnamed x13 -> x0, local copies, waits for them, and re-layouts: 5.84 us -> none
where the time goes in v3:
time: 164 us
  Pallas kernels  163 us (99%)
    pallas_call x1, Pallas kernels, local(): pl.pallas_call(output_kernel, out_shape=(sds((SPAN, INNER)), sds((SPAN, S...  82.8 us
    pallas_call x1, Pallas kernels, local(): pl.pallas_call(mixer_kernel, out_shape=(sds((SPAN, INNER)), sds((SPAN, ST...  80.6 us

profile of v3, /device:TPU:0, one launch (start us, length us, event | category | flops | bytes accessed | tf_op | source)
XLA Modules:
  0.0 164.0 jit_solution(2786752202027967250)
XLA Ops:
  0.6 80.6 %mixer.1 = (f32[256,2048]{1,0:T(8,128)}, f32[256,128]{1,0:T(8,128)}, f32[256,128]{1,0:T(8,128)}, f32[32,256]{1,0:T(8,128)}, f32[32,128]{1,0:T(8,128)}, /*index=5*/f32[64,1024]{1,0:T(8,128)}) custom-call(bf16[256,2048]{1,0:T(8,128)(2,1)} %bitcast.13, bf16[256,128]{1,0:T(8,128)(2,1)} %bitcast.15, bf16[256,128]{1,0:T(8,128)(2,1)} %bitcast.16, ...), custom_call_target="tpu_custom_call" | custom-call | tf_op jit(solution)/shard_map/mixer/pallas_call | solution.py:524
  81.2 82.8 %output.1 = (f32[256,2048]{1,0:T(8,128)}, f32[256,128]{1,0:T(8,128)}, f32[256,128]{1,0:T(8,128)}, f32[32,256]{1,0:T(8,128)}, f32[1,32]{1,0:T(1,128)}, /*index=5*/f32[1,32]{1,0:T(1,128)}, f32[64,1024]{1,0:T(8,128)}) custom-call(f32[256,2048]{1,0:T(8,128)} %get-tuple-element.20.gv, f32[256,128]{1,0:T(8,128)} %get-tuple-element.21.gk, ...), custom_call_target="tpu_custom_call" | custom-call | tf_op jit(solution)/shard_map/output/pallas_call | solution.py:561

commit v4 on v3

--- a/solution.py
+++ b/solution.py
@@ -171,6 +171,26 @@
         return carry
 
     lax.fori_loop(0, CHIPS, local_state, 0)
+    pl.semaphore_wait(barrier, CHIPS + 3)
+    wait(start([core_copy(d_ref, dp, 0), core_copy(t_ref.at[:, 1 - c], tp, 1)]))
+
+    def combine_forward(i, carry):
+        d0, d1 = both(d_ref[i, c], dp[i, c])
+        t0, t1 = both(t_ref[i, c], tp[i])
+        upf[i, 0:8] = d1[None] * t0 + t1
+        upf[i, 8] = d0 * d1
+        return carry
+
+    lax.fori_loop(0, CHIPS, combine_forward, 0)
+
+    forward_out = start(spread(upf, gotf, 0))
+    gotf[g] = upf[g]
+
+    wait(loads[4:])
+    f_og[...] = og_ref[...].astype(F32)
+    f_q[...] = q_ref[...].astype(F32)
+    early = start([core_copy(f_og, r_og, 3), core_copy(f_q, r_q, 4), core_copy(erow, r_e, 5)])
+
     def cotangent(m, carry):
         rows = pl.ds(pl.multiple_of(m * 512, 512), 512)
         gbuf[...] = nt(w_ref[rows, :], og_ref[...])
@@ -183,42 +203,8 @@
             e_ref[i] = (nn(high, q_ref[...]) + nn(low, q_ref[...])).reshape(2, 8, 8, STATE)
         return carry
 
-    wait(loads[4:])
     lax.fori_loop(0, 4, cotangent, 0)
-    pl.semaphore_wait(barrier, CHIPS + 3)
-    swaps = start([
-        core_copy(d_ref, dp, 0), core_copy(t_ref.at[:, 1 - c], tp, 1), core_copy(e_ref.at[:, 1 - c], ep, 2)
-    ])
-    wait(swaps[:2])
-
-    def combine_forward(i, carry):
-        d0, d1 = both(d_ref[i, c], dp[i, c])
-        t0, t1 = both(t_ref[i, c], tp[i])
-        upf[i, 0:8] = d1[None] * t0 + t1
-        upf[i, 8] = d0 * d1
-        return carry
-
-    lax.fori_loop(0, CHIPS, combine_forward, 0)
-
-    forward_out = start(spread(upf, gotf, 0))
-    gotf[g] = upf[g]
-
-    wait(swaps[2:])
-
-    def combine_backward(i, carry):
-        d0, d1 = both(d_ref[i, c], dp[i, c])
-        e0, e1 = both(e_ref[i, c], ep[i])
-        upb[i, 0:8] = e0 + d0[None] * e1
-        upb[i, 8] = d0 * d1
-        return carry
-
-    lax.fori_loop(0, CHIPS, combine_backward, 0)
-    backward_out = start(spread(upb, gotb, 2))
-    gotb[g] = upb[g]
-
-    f_og[...] = og_ref[...].astype(F32)
-    f_q[...] = q_ref[...].astype(F32)
-    early = start([core_copy(f_og, r_og, 3), core_copy(f_q, r_q, 4), core_copy(erow, r_e, 5)])
+    swap_e = start([core_copy(e_ref.at[:, 1 - c], ep, 2)])
 
     skrow[...] = jnp.broadcast_to(column(sk_ref[...]), (HEADS, SPAN))
     jj = lax.broadcasted_iota(jnp.int32, (SPAN, SPAN), 0)
@@ -284,7 +270,20 @@
         row_sums(xrow, gf * xf, i)
         return carry
 
-    lax.fori_loop(0, 6, inside, 0)
+    lax.fori_loop(0, 3, inside, 0)
+    wait(swap_e)
+
+    def combine_backward(i, carry):
+        d0, d1 = both(d_ref[i, c], dp[i, c])
+        e0, e1 = both(e_ref[i, c], ep[i])
+        upb[i, 0:8] = e0 + d0[None] * e1
+        upb[i, 8] = d0 * d1
+        return carry
+
+    lax.fori_loop(0, CHIPS, combine_backward, 0)
+    backward_out = start(spread(upb, gotb, 2))
+    gotb[g] = upb[g]
+    lax.fori_loop(3, 6, inside, 0)
     wait(forward_out)
     carried = jnp.zeros((8, 8, STATE), F32)
     for i in range(CHIPS):
@@ -292,7 +291,12 @@
         carried = gotf[i, 8][None] * carried + gotf[i, 0:8]
     forward_in = start(spread(backf, homef, 1))
     homef[g] = backf[g]
-    lax.fori_loop(6, 11, inside, 0)
+    lax.fori_loop(6, CHIPS, inside, 0)
+    wait(early)
+    swap_y = start([core_copy(ysum.at[:, 1 - c], yp, 6)])
+    rhs[:SPAN] = og_ref[...]
+    rhs[SPAN:] = r_og[...].astype(BF16)
+    s_mine, s_other = q_ref[...], r_q[...].astype(BF16)
     wait(backward_out)
     carried = jnp.zeros((8, 8, STATE), F32)
     for i in range(CHIPS - 1, -1, -1):
@@ -300,12 +304,6 @@
         carried = gotb[i, 8][None] * carried + gotb[i, 0:8]
     backward_in = start(spread(backb, homeb, 3))
     homeb[g] = backb[g]
-    lax.fori_loop(11, CHIPS, inside, 0)
-    wait(early)
-    swap_y = start([core_copy(ysum.at[:, 1 - c], yp, 6)])
-    rhs[:SPAN] = og_ref[...]
-    rhs[SPAN:] = r_og[...].astype(BF16)
-    s_mine, s_other = q_ref[...], r_q[...].astype(BF16)
     wait(swap_y)
     wait(forward_in)
 
@@ -489,20 +487,26 @@
 
 
 def output_kernel(
-    gv, gk, gq, gs, small, gw, gv_out, gk_out, gq_out, gs_out, decay_out, skip_out, gw_out, sem
+    gv, gk, gq, gs, small, gw, gv_out, gk_out, gq_out, gs_out, decay_out, skip_out, gw_out,
+    vv, vk, vq, vs, vw, into, out,
 ):
     quarter = SPAN // 4
-    pairs = [(gv.at[pl.ds(n * quarter, quarter)], gv_out.at[pl.ds(n * quarter, quarter)]) for n in range(4)]
-    pairs += [(gk, gk_out), (gq, gq_out), (gs, gs_out), (gw, gw_out)]
-    copies = [pltpu.make_async_copy(a, b, sem.at[n]) for n, (a, b) in enumerate(pairs)]
-    for n in copies:
+    parts = [pl.ds(n * quarter, quarter) for n in range(4)]
+    moves = [(gv.at[n], vv.at[n], gv_out.at[n]) for n in parts]
+    moves += [(gw, vw, gw_out), (gk, vk, gk_out), (gq, vq, gq_out), (gs, vs, gs_out)]
+    reads = [pltpu.make_async_copy(a, b, into.at[n]) for n, (a, b, _) in enumerate(moves)]
+    writes = [pltpu.make_async_copy(b, a, out.at[n]) for n, (_, b, a) in enumerate(moves)]
+    for n in reads:
         n.start()
     i = lax.broadcasted_iota(jnp.int32, (HEADS, HEADS), 0)
     j = lax.broadcasted_iota(jnp.int32, (HEADS, HEADS), 1)
     for n, ref in enumerate((decay_out, skip_out)):
         whole = jnp.broadcast_to(small[:, n : n + 1], (HEADS, HEADS))
         ref[...] = jnp.sum(jnp.where(i == j, whole, 0.0), axis=0, keepdims=True)
-    for n in copies:
+    for a, b in zip(reads, writes):
+        a.wait()
+        b.start()
+    for n in writes:
         n.wait()
 
 
@@ -566,7 +570,10 @@
         ),
         in_specs=[anywhere] * 4 + [inside, anywhere],
         out_specs=(anywhere,) * 4 + (inside,) * 2 + (anywhere,),
-        scratch_shapes=[dma((8,))],
+        scratch_shapes=[
+            vm((SPAN, INNER), F32), vm((SPAN, STATE), F32), vm((SPAN, STATE), F32), row,
+            vm((64, MODEL), F32), dma((8,)), dma((8,)),
+        ],
         compiler_params=pltpu.CompilerParams(vmem_limit_bytes=60 * 1024 * 1024),
         name="output",
     )(*made)

time: 164 us -> 81.7 us (0.50)
  Pallas kernels: 163 us -> 80.9 us
    pallas_call x1, Pallas kernels: 82.8 us -> 3.89 us  [local(): pl.pallas_call(output_kernel, out_shape=(sds((SPAN, INNER)), sds((SPAN, S...]
    pallas_call x1, Pallas kernels: 80.6 us -> 77 us  [local(): pl.pallas_call(mixer_kernel, out_shape=(sds((SPAN, INNER)), sds((SPAN, ST...]
where the time goes in v4:
time: 81.7 us; the launch traced here: 81.5 us
  Pallas kernels  80.9 us (99%)
    pallas_call x1, Pallas kernels, local(): pl.pallas_call(mixer_kernel, out_shape=(sds((SPAN, INNER)), sds((SPAN, ST...  77 us
    pallas_call x1, Pallas kernels, local(): pl.pallas_call(output_kernel, out_shape=(sds((SPAN, INNER)), sds((SPAN, S...  3.89 us

profile of v4, /device:TPU:0, one launch (start us, length us, event | category | flops | bytes accessed | tf_op | source)
XLA Modules:
  0.0 81.5 jit_solution(3768886514610976251)
XLA Ops:
  0.6 77.0 %mixer.1 = (f32[256,2048]{1,0:T(8,128)}, f32[256,128]{1,0:T(8,128)}, f32[256,128]{1,0:T(8,128)}, f32[32,256]{1,0:T(8,128)}, f32[32,128]{1,0:T(8,128)}, /*index=5*/f32[64,1024]{1,0:T(8,128)}) custom-call(bf16[256,2048]{1,0:T(8,128)(2,1)} %bitcast.13, bf16[256,128]{1,0:T(8,128)(2,1)} %bitcast.15, bf16[256,128]{1,0:T(8,128)(2,1)} %bitcast.16, ...), custom_call_target="tpu_custom_call" | custom-call | tf_op jit(solution)/shard_map/mixer/pallas_call | solution.py:528
  77.6 3.9 %output.1 = (f32[256,2048]{1,0:T(8,128)}, f32[256,128]{1,0:T(8,128)}, f32[256,128]{1,0:T(8,128)}, f32[32,256]{1,0:T(8,128)}, f32[1,32]{1,0:T(1,128)}, /*index=5*/f32[1,32]{1,0:T(1,128)}, f32[64,1024]{1,0:T(8,128)}) custom-call(f32[256,2048]{1,0:T(8,128)} %get-tuple-element.20.gv, f32[256,128]{1,0:T(8,128)} %get-tuple-element.21.gk, ...), custom_call_target="tpu_custom_call" | custom-call | tf_op jit(solution)/shard_map/output/pallas_call | solution.py:565

commit v5 on v4

--- a/solution.py
+++ b/solution.py
@@ -75,7 +75,7 @@
     s_ref, ds_ref, give_s, give_d,
     scores, acc, qacc, kacc, ysum, yp, dxt, gv_ref,
     f_og, r_og, f_q, r_q, r_e, rhs, dw0, dw1, dw2,
-    a0, a1, a2, b0, b1, b2, ra0, ra1, ra2, rb0, rb1, rb2, rc0, rc1, rc2, w0, w1, w2,
+    a0, a1, a2, b0, b1, b2, ra0, ra1, ra2, rb0, rb1, rb2, rc0, rc1, rc2, w0, w1, w2, q0, q1, q2,
     s_core, s_x, s_y, s_z,
     in_sem, out_sem, core_send, core_recv, plane_send, plane_recv,
     first_send, first_recv, send, recv,
@@ -308,19 +308,32 @@
     wait(forward_in)
 
     recv_a, recv_b, recv_c = (ra0, ra1, ra2), (rb0, rb1, rb2), (rc0, rc1, rc2)
-    first = ([], [], [])
-
-    def first_copy(axis, d, src, dst, n):
+    first, used = ([], [], []), []
+    low, high = pl.ds(0, 2), pl.ds(2, 2)
+
+    def first_copy(axis, d, src, dst):
+        n = len(used)
+        used.append(n)
         return pltpu.make_async_remote_copy(
             src_ref=src, dst_ref=dst, send_sem=first_send.at[n], recv_sem=first_recv.at[n],
             device_id=device(axis, other(axis, d)), device_id_type=MESH,
         )
 
+    def send_far(axis, piece, relay):
+        return start([first_copy(axis, 1, piece.at[low], relay.at[0]), first_copy(axis, 3, piece.at[high], relay.at[1])])
+
+    def send_sums(axis, far, up, down, relay, got0, got1):
+        wait(far)
+        relay[0] = relay[0] + up[:2]
+        relay[1] = relay[1] + down[2:]
+        return start([first_copy(axis, 1, relay.at[0], got0.at[low]), first_copy(axis, 3, relay.at[1], got1.at[high])])
+
     def across(states, queries):
         high, low = split(states)
         return nt(high, queries) + nt(low, queries)
 
-    for step, turn in enumerate((2, 1, 3, 0)):
+    fars = []
+    for turn in (2, 1, 3, 0):
         m = other("x", turn)
         own_states, other_states, own_rows, other_rows, own_y, other_y = [], [], [], [], [], []
         for n in range(4):
@@ -351,21 +364,30 @@
         for n in range(4):
             dw1[m, n, :, :, :384] = whole[:, n, 0, :, 640:]
             dw1[m, n, :, :, 384:] = whole[:, n, 1, :, :384]
-        copies = []
-        if turn:
-            cp = first_copy("x", turn, dw0.at[m], ra0.at[turn - 1], turn - 1)
-            first[0].append(cp)
-            copies.append(cp)
-        for d in range(1, 4):
-            cp = first_copy("y", d, dw1.at[m, other("y", d)], ra1.at[d - 1, m], 3 + step * 3 + d - 1)
-            first[1].append(cp)
-            copies.append(cp)
-            cp = first_copy("z", d, dw2.at[m, other("z", d)], ra2.at[d - 1, m], 15 + step * 3 + d - 1)
-            first[2].append(cp)
-            copies.append(cp)
-        start(copies)
+        if turn == 2:
+            far_x = send_far("x", dw0.at[m], q0)
+        elif turn == 1:
+            first[0].extend(start([first_copy("x", 1, dw0.at[m, high], ra0.at[0, high])]))
+        elif turn == 3:
+            first[0].extend(start([first_copy("x", 3, dw0.at[m, low], ra0.at[1, low])]))
+        pairs = []
+        for p, axis, dw, ra, q in ((1, "y", dw1, ra1, q1), (2, "z", dw2, ra2, q2)):
+            pairs.append(send_far(axis, dw.at[m, other(axis, 2)], q.at[m]))
+            first[p].extend(start([
+                first_copy(axis, 1, dw.at[m, other(axis, 1), high], ra.at[0, m, high]),
+                first_copy(axis, 3, dw.at[m, other(axis, 3), low], ra.at[1, m, low]),
+            ]))
+        fars.append((m, pairs))
+
+    def relay_sums(step):
+        m, pairs = fars[step]
+        for far, (p, axis, dw, ra, q) in zip(pairs, ((1, "y", dw1, ra1, q1), (2, "z", dw2, ra2, q2))):
+            up, down = dw[m, other(axis, 1)], dw[m, other(axis, 3)]
+            first[p].extend(send_sums(axis, far, up, down, q.at[m], ra.at[0, m], ra.at[1, m]))
 
     swap_s = start([core_copy(give_s, s_ref.at[:, c], 7)])
+    relay_sums(0)
+    first[0].extend(send_sums("x", far_x, dw0[other("x", 1)], dw0[other("x", 3)], q0, ra0.at[0], ra0.at[1]))
     wait(backward_in)
 
     def finish_backward(i, carry):
@@ -378,6 +400,7 @@
 
     lax.fori_loop(0, CHIPS, finish_backward, 0)
     swap_d = start([core_copy(give_d, ds_ref.at[:, c], 8)])
+    relay_sums(1)
     wait(swap_s)
     wait(swap_d)
 
@@ -407,7 +430,10 @@
             vrow[h, :] = jnp.sum(sd[part], axis=0, keepdims=True)
         return carry
 
-    lax.fori_loop(0, CHIPS, outside, 0)
+    lax.fori_loop(0, 7, outside, 0)
+    relay_sums(2)
+    relay_sums(3)
+    lax.fori_loop(7, CHIPS, outside, 0)
     store = pltpu.make_async_copy(gv_ref, gv_hbm, out_sem)
     store.start()
     dst = jnp.where(causal, acc[...], 0.0).astype(BF16)
@@ -459,7 +485,7 @@
         wait(first[p])
         got = recv_a[p]
         mine = parts[p][pick(layouts[p], order[0], coord[order[0]])]
-        sums_a[p][...] = (mine + got[0]) + (got[1] + got[2])
+        sums_a[p][...] = mine + (got[0] + got[1])
         rest = layouts[p].replace(order[0], "")
         second.append(reduce_start(sums_a[p], rest, order[1], recv_b[p], p))
     small = small_start("y", s_y, small_sum(small, s_x), 10)
@@ -488,21 +514,26 @@
 
 def output_kernel(
     gv, gk, gq, gs, small, gw, gv_out, gk_out, gq_out, gs_out, decay_out, skip_out, gw_out,
-    vv, vk, vq, vs, vw, into, out,
+    vv, vk, vq, vs, vm, vw, vd, vp, into, out,
 ):
-    quarter = SPAN // 4
-    parts = [pl.ds(n * quarter, quarter) for n in range(4)]
+    size = SPAN // 8
+    parts = [pl.ds(n * size, size) for n in range(8)]
     moves = [(gv.at[n], vv.at[n], gv_out.at[n]) for n in parts]
     moves += [(gw, vw, gw_out), (gk, vk, gk_out), (gq, vq, gq_out), (gs, vs, gs_out)]
+    first = pltpu.make_async_copy(small, vm, into.at[12])
     reads = [pltpu.make_async_copy(a, b, into.at[n]) for n, (a, b, _) in enumerate(moves)]
     writes = [pltpu.make_async_copy(b, a, out.at[n]) for n, (_, b, a) in enumerate(moves)]
+    writes += [pltpu.make_async_copy(vd, decay_out, out.at[12]), pltpu.make_async_copy(vp, skip_out, out.at[13])]
+    first.start()
     for n in reads:
         n.start()
+    first.wait()
     i = lax.broadcasted_iota(jnp.int32, (HEADS, HEADS), 0)
     j = lax.broadcasted_iota(jnp.int32, (HEADS, HEADS), 1)
-    for n, ref in enumerate((decay_out, skip_out)):
-        whole = jnp.broadcast_to(small[:, n : n + 1], (HEADS, HEADS))
+    for n, ref in enumerate((vd, vp)):
+        whole = jnp.broadcast_to(vm[:, n : n + 1], (HEADS, HEADS))
         ref[...] = jnp.sum(jnp.where(i == j, whole, 0.0), axis=0, keepdims=True)
+        writes[12 + n].start()
     for a, b in zip(reads, writes):
         a.wait()
         b.start()
@@ -548,14 +579,15 @@
             row, vm((2 * SPAN, MODEL), BF16), *[vm((4, 4, 4, 8, w), F32) for w in wides],
             *[vm((4, 4, 8, w), F32) for w in wides],
             *[vm((4, 8, w), F32) for w in wides],
-            *[vm((3, 4, 4, 8, w), F32) for w in wides],
+            *[vm((2, 4, 4, 8, w), F32) for w in wides],
             *[vm((3, 4, 8, w), F32) for w in wides],
             *[vm((3, 8, w), F32) for w in wides],
             *[vm((4, 8, w), F32) for w in wides],
+            vm((2, 2, 4, 8, wides[0]), F32), vm((4, 2, 2, 8, wides[1]), F32), vm((4, 2, 2, 8, wides[2]), F32),
             vm((2, HEADS, 128), F32),
             *[vm((4, HEADS, 128), F32)] * 3,
             dma((8,)), dma, dma((10,)), dma((10,)), dma((4, CHIPS)), dma((4, CHIPS)),
-            dma((27,)), dma((27,)), dma((12, 3)), dma((12, 3)),
+            dma((54,)), dma((54,)), dma((12, 3)), dma((12, 3)),
         ],
         compiler_params=pltpu.CompilerParams(
             vmem_limit_bytes=60 * 1024 * 1024, collective_id=0, has_side_effects=True
@@ -568,11 +600,12 @@
             sds((SPAN, INNER)), sds((SPAN, STATE)), sds((SPAN, STATE)), sds((HEADS, SPAN)),
             sds((1, HEADS)), sds((1, HEADS)), sds((64, MODEL)),
         ),
-        in_specs=[anywhere] * 4 + [inside, anywhere],
-        out_specs=(anywhere,) * 4 + (inside,) * 2 + (anywhere,),
+        in_specs=[anywhere] * 6,
+        out_specs=(anywhere,) * 7,
         scratch_shapes=[
             vm((SPAN, INNER), F32), vm((SPAN, STATE), F32), vm((SPAN, STATE), F32), row,
-            vm((64, MODEL), F32), dma((8,)), dma((8,)),
+            vm((HEADS, 128), F32), vm((64, MODEL), F32), vm((1, HEADS), F32), vm((1, HEADS), F32),
+            dma((13,)), dma((14,)),
         ],
         compiler_params=pltpu.CompilerParams(vmem_limit_bytes=60 * 1024 * 1024),
         name="output",

time: 81.7 us -> 77.5 us (0.949)
  Pallas kernels: 80.9 us -> 76.7 us
    pallas_call x1, Pallas kernels: 77 us -> 74 us  [local(): pl.pallas_call(mixer_kernel, out_shape=(sds((SPAN, INNER)), sds((SPAN, ST...]
    pallas_call x1, Pallas kernels: 3.89 us -> 2.68 us  [local(): pl.pallas_call(output_kernel, out_shape=(sds((SPAN, INNER)), sds((SPAN, S...]
where the time goes in v5:
time: 77.5 us; the launch traced here: 77.3 us
  Pallas kernels  76.7 us (99%)
    pallas_call x1, Pallas kernels, local(): pl.pallas_call(mixer_kernel, out_shape=(sds((SPAN, INNER)), sds((SPAN, ST...  74 us
    pallas_call x1, Pallas kernels, local(): pl.pallas_call(output_kernel, out_shape=(sds((SPAN, INNER)), sds((SPAN, S...  2.68 us

profile of v5, /device:TPU:0, one launch (start us, length us, event | category | flops | bytes accessed | tf_op | source)
XLA Modules:
  0.0 77.3 jit_solution(13441281839890186361)
XLA Ops:
  0.6 74.0 %mixer.1 = (f32[256,2048]{1,0:T(8,128)}, f32[256,128]{1,0:T(8,128)}, f32[256,128]{1,0:T(8,128)}, f32[32,256]{1,0:T(8,128)}, f32[32,128]{1,0:T(8,128)}, /*index=5*/f32[64,1024]{1,0:T(8,128)}) custom-call(bf16[256,2048]{1,0:T(8,128)(2,1)} %bitcast.13, bf16[256,128]{1,0:T(8,128)(2,1)} %bitcast.15, bf16[256,128]{1,0:T(8,128)(2,1)} %bitcast.16, ...), custom_call_target="tpu_custom_call" | custom-call | tf_op jit(solution)/shard_map/mixer/pallas_call | solution.py:559
  74.6 2.7 %output.1 = (f32[256,2048]{1,0:T(8,128)}, f32[256,128]{1,0:T(8,128)}, f32[256,128]{1,0:T(8,128)}, f32[32,256]{1,0:T(8,128)}, f32[1,32]{1,0:T(1,128)}, /*index=5*/f32[1,32]{1,0:T(1,128)}, f32[64,1024]{1,0:T(8,128)}) custom-call(f32[256,2048]{1,0:T(8,128)} %get-tuple-element.20.gv, f32[256,128]{1,0:T(8,128)} %get-tuple-element.21.gk, ...), custom_call_target="tpu_custom_call" | custom-call | tf_op jit(solution)/shard_map/output/pallas_call | solution.py:597

commit v6 on v5

--- a/solution.py
+++ b/solution.py
@@ -57,7 +57,7 @@
     return high, (v - high.astype(F32)).astype(BF16)
 
 
-PARTS = ((640, "xyz"), (768, "yzx"), (640, "zxy"))
+PARTS = ((768, "xyz"), (640, "yzx"), (640, "zxy"))
 HALF = SPAN // 2
 
 
@@ -270,7 +270,6 @@
         row_sums(xrow, gf * xf, i)
         return carry
 
-    lax.fori_loop(0, 3, inside, 0)
     wait(swap_e)
 
     def combine_backward(i, carry):
@@ -283,7 +282,6 @@
     lax.fori_loop(0, CHIPS, combine_backward, 0)
     backward_out = start(spread(upb, gotb, 2))
     gotb[g] = upb[g]
-    lax.fori_loop(3, 6, inside, 0)
     wait(forward_out)
     carried = jnp.zeros((8, 8, STATE), F32)
     for i in range(CHIPS):
@@ -291,7 +289,7 @@
         carried = gotf[i, 8][None] * carried + gotf[i, 0:8]
     forward_in = start(spread(backf, homef, 1))
     homef[g] = backf[g]
-    lax.fori_loop(6, CHIPS, inside, 0)
+    lax.fori_loop(0, CHIPS, inside, 0)
     wait(early)
     swap_y = start([core_copy(ysum.at[:, 1 - c], yp, 6)])
     rhs[:SPAN] = og_ref[...]
@@ -359,11 +357,11 @@
         right = join(other_y) + across(join(other_states), s_other) * join(other_rows)
         lhs = jnp.concatenate([left.astype(BF16), right.astype(BF16)], axis=1)
         whole = nn(lhs, rhs[...]).reshape(4, 4, 2, 8, MODEL)
-        dw0[m] = whole[:, :, 0, :, :640]
+        dw0[m] = whole[:, :, 0, :, :768]
         dw2[m] = whole[:, :, 1, :, 384:]
         for n in range(4):
-            dw1[m, n, :, :, :384] = whole[:, n, 0, :, 640:]
-            dw1[m, n, :, :, 384:] = whole[:, n, 1, :, :384]
+            dw1[m, n, :, :, :256] = whole[:, n, 0, :, 768:]
+            dw1[m, n, :, :, 256:] = whole[:, n, 1, :, :384]
         if turn == 2:
             far_x = send_far("x", dw0.at[m], q0)
         elif turn == 1:
@@ -388,6 +386,9 @@
     swap_s = start([core_copy(give_s, s_ref.at[:, c], 7)])
     relay_sums(0)
     first[0].extend(send_sums("x", far_x, dw0[other("x", 1)], dw0[other("x", 3)], q0, ra0.at[0], ra0.at[1]))
+    relay_sums(1)
+    relay_sums(2)
+    relay_sums(3)
     wait(backward_in)
 
     def finish_backward(i, carry):
@@ -400,7 +401,6 @@
 
     lax.fori_loop(0, CHIPS, finish_backward, 0)
     swap_d = start([core_copy(give_d, ds_ref.at[:, c], 8)])
-    relay_sums(1)
     wait(swap_s)
     wait(swap_d)
 
@@ -430,10 +430,43 @@
             vrow[h, :] = jnp.sum(sd[part], axis=0, keepdims=True)
         return carry
 
-    lax.fori_loop(0, 7, outside, 0)
-    relay_sums(2)
-    relay_sums(3)
-    lax.fori_loop(7, CHIPS, outside, 0)
+    lax.fori_loop(0, 4, outside, 0)
+    lax.fori_loop(4, 8, outside, 0)
+    def reach(axis, d, src, dst, n):
+        return pltpu.make_async_remote_copy(
+            src_ref=src, dst_ref=dst, send_sem=send.at[n, d - 1], recv_sem=recv.at[n, d - 1],
+            device_id=device(axis, other(axis, d)), device_id_type=MESH,
+        )
+
+    def small_start(axis, buf, value, n):
+        buf[coord[axis]] = value
+        mine = buf.at[coord[axis]]
+        return start([reach(axis, d, mine, mine, n) for d in range(1, 4)])
+
+    def small_sum(copies, buf):
+        wait(copies)
+        return (buf[0] + buf[1]) + (buf[2] + buf[3])
+
+    def pick(dims, axis, value):
+        return tuple(value if n == axis else slice(None) for n in dims)
+
+    def reduce_start(src, dims, axis, dst, n):
+        return start([
+            reach(axis, d, src.at[pick(dims, axis, other(axis, d))], dst.at[d - 1], n) for d in range(1, 4)
+        ])
+
+    parts, sums_a, sums_b, rows = (dw0, dw1, dw2), (a0, a1, a2), (b0, b1, b2), (w0, w1, w2)
+    layouts = ("xzy", "xyz", "xzy")
+    second, third, last = [], [], []
+    for p, (_, order) in enumerate(PARTS):
+        wait(first[p])
+        got = recv_a[p]
+        mine = parts[p][pick(layouts[p], order[0], coord[order[0]])]
+        sums_a[p][...] = mine + (got[0] + got[1])
+        rest = layouts[p].replace(order[0], "")
+        second.append(reduce_start(sums_a[p], rest, order[1], recv_b[p], p))
+
+    lax.fori_loop(8, CHIPS, outside, 0)
     store = pltpu.make_async_copy(gv_ref, gv_hbm, out_sem)
     store.start()
     dst = jnp.where(causal, acc[...], 0.0).astype(BF16)
@@ -453,42 +486,7 @@
     lane = lax.broadcasted_iota(jnp.int32, (HEADS, 128), 1)
     s_core[c] = jnp.where(lane == 0, g_decay, jnp.where(lane == 1, g_skip, 0.0))
     wait(start([core_copy(s_core.at[c], s_core.at[c], 9)]))
-
-    def reach(axis, d, src, dst, n):
-        return pltpu.make_async_remote_copy(
-            src_ref=src, dst_ref=dst, send_sem=send.at[n, d - 1], recv_sem=recv.at[n, d - 1],
-            device_id=device(axis, other(axis, d)), device_id_type=MESH,
-        )
-
-    def small_start(axis, buf, value, n):
-        buf[coord[axis]] = value
-        mine = buf.at[coord[axis]]
-        return start([reach(axis, d, mine, mine, n) for d in range(1, 4)])
-
-    def small_sum(copies, buf):
-        wait(copies)
-        return (buf[0] + buf[1]) + (buf[2] + buf[3])
-
-    def pick(dims, axis, value):
-        return tuple(value if n == axis else slice(None) for n in dims)
-
-    def reduce_start(src, dims, axis, dst, n):
-        return start([
-            reach(axis, d, src.at[pick(dims, axis, other(axis, d))], dst.at[d - 1], n) for d in range(1, 4)
-        ])
-
-    parts, sums_a, sums_b, rows = (dw0, dw1, dw2), (a0, a1, a2), (b0, b1, b2), (w0, w1, w2)
-    layouts = ("xzy", "xyz", "xzy")
     small = small_start("x", s_x, s_core[0] + s_core[1], 9)
-    second, third, last = [], [], []
-    for p, (_, order) in enumerate(PARTS):
-        wait(first[p])
-        got = recv_a[p]
-        mine = parts[p][pick(layouts[p], order[0], coord[order[0]])]
-        sums_a[p][...] = mine + (got[0] + got[1])
-        rest = layouts[p].replace(order[0], "")
-        second.append(reduce_start(sums_a[p], rest, order[1], recv_b[p], p))
-    small = small_start("y", s_y, small_sum(small, s_x), 10)
     for p, (_, order) in enumerate(PARTS):
         wait(second[p])
         rest = layouts[p].replace(order[0], "")
@@ -496,19 +494,20 @@
         mine = sums_a[p][pick(rest, order[1], coord[order[1]])]
         sums_b[p][...] = (mine + got[0]) + (got[1] + got[2])
         third.append(reduce_start(sums_b[p], order[2], order[2], recv_c[p], 3 + p))
-    small = small_start("z", s_z, small_sum(small, s_y), 11)
+    small = small_start("y", s_y, small_sum(small, s_x), 10)
     for p, (_, order) in enumerate(PARTS):
         wait(third[p])
         got = recv_c[p]
         rows[p][y] = (sums_b[p][coord[order[2]]] + got[0]) + (got[1] + got[2])
         last.extend(start([reach("y", d, rows[p].at[y], rows[p].at[y], 6 + p) for d in range(1, 4)]))
+    small = small_start("z", s_z, small_sum(small, s_y), 11)
     smo_ref[...] = small_sum(small, s_z)
     store.wait()
     wait(last)
     for n in range(4):
-        gw_ref[16 * n : 16 * n + 8, :640] = w0[n]
-        gw_ref[16 * n : 16 * n + 8, 640:] = w1[n, :, :384]
-        gw_ref[16 * n + 8 : 16 * n + 16, :384] = w1[n, :, 384:]
+        gw_ref[16 * n : 16 * n + 8, :768] = w0[n]
+        gw_ref[16 * n : 16 * n + 8, 768:] = w1[n, :, :256]
+        gw_ref[16 * n + 8 : 16 * n + 16, :384] = w1[n, :, 256:]
         gw_ref[16 * n + 8 : 16 * n + 16, 384:] = w2[n]
 
 

time: 77.5 us -> 76.2 us (0.983)
  Pallas kernels: 76.7 us -> 75.4 us
    pallas_call x1, Pallas kernels: 74 us -> 72.7 us  [local(): pl.pallas_call(mixer_kernel, out_shape=(sds((SPAN, INNER)), sds((SPAN, ST...]
where the time goes in v6:
time: 76.2 us; the launch traced here: 76 us
  Pallas kernels  75.4 us (99%)
    pallas_call x1, Pallas kernels, local(): pl.pallas_call(mixer_kernel, out_shape=(sds((SPAN, INNER)), sds((SPAN, ST...  72.7 us
    pallas_call x1, Pallas kernels, local(): pl.pallas_call(output_kernel, out_shape=(sds((SPAN, INNER)), sds((SPAN, S...  2.68 us

profile of v6, /device:TPU:0, one launch (start us, length us, event | category | flops | bytes accessed | tf_op | source)
XLA Modules:
  0.0 76.0 jit_solution(12954236537920084913)
XLA Ops:
  0.6 72.7 %mixer.1 = (f32[256,2048]{1,0:T(8,128)}, f32[256,128]{1,0:T(8,128)}, f32[256,128]{1,0:T(8,128)}, f32[32,256]{1,0:T(8,128)}, f32[32,128]{1,0:T(8,128)}, /*index=5*/f32[64,1024]{1,0:T(8,128)}) custom-call(bf16[256,2048]{1,0:T(8,128)(2,1)} %bitcast.13, bf16[256,128]{1,0:T(8,128)(2,1)} %bitcast.15, bf16[256,128]{1,0:T(8,128)(2,1)} %bitcast.16, ...), custom_call_target="tpu_custom_call" | custom-call | tf_op jit(solution)/shard_map/mixer/pallas_call | solution.py:558
  73.4 2.7 %output.1 = (f32[256,2048]{1,0:T(8,128)}, f32[256,128]{1,0:T(8,128)}, f32[256,128]{1,0:T(8,128)}, f32[32,256]{1,0:T(8,128)}, f32[1,32]{1,0:T(1,128)}, /*index=5*/f32[1,32]{1,0:T(1,128)}, f32[64,1024]{1,0:T(8,128)}) custom-call(f32[256,2048]{1,0:T(8,128)} %get-tuple-element.20.gv, f32[256,128]{1,0:T(8,128)} %get-tuple-element.21.gk, ...), custom_call_target="tpu_custom_call" | custom-call | tf_op jit(solution)/shard_map/output/pallas_call | solution.py:596

commit v7 on v6

--- a/solution.py
+++ b/solution.py
@@ -67,13 +67,13 @@
 
 def mixer_kernel(
     x_hbm, k_hbm, q_hbm, dt_hbm, dl_hbm, sk_hbm, w_hbm, og_hbm,
-    gv_hbm, gk_ref, gq_ref, gs_ref, smo_ref, gw_ref,
+    gv_hbm, gk_hbm, gq_hbm, gs_hbm, smo_hbm, gw_hbm,
     x_ref, k_ref, q_ref, dt_ref, dl_ref, sk_ref, w_ref, og_ref,
     run2, crow, wrow, erow, skrow, frow, rrow, urow, xrow, vrow,
     gbuf, xt_ref, gt_ref, t_ref, e_ref, d_ref, tp, ep, dp,
     upf, gotf, backf, homef, upb, gotb, backb, homeb,
     s_ref, ds_ref, give_s, give_d,
-    scores, acc, qacc, kacc, ysum, yp, dxt, gv_ref,
+    scores, acc, qacc, kacc, ysum, yp, dxt, gv_ref, gk_ref, gq_ref, gs_ref, smo_ref, gw_ref,
     f_og, r_og, f_q, r_q, r_e, rhs, dw0, dw1, dw2,
     a0, a1, a2, b0, b1, b2, ra0, ra1, ra2, rb0, rb1, rb2, rc0, rc1, rc2, w0, w1, w2, q0, q1, q2,
     s_core, s_x, s_y, s_z,
@@ -467,8 +467,13 @@
         second.append(reduce_start(sums_a[p], rest, order[1], recv_b[p], p))
 
     lax.fori_loop(8, CHIPS, outside, 0)
-    store = pltpu.make_async_copy(gv_ref, gv_hbm, out_sem)
-    store.start()
+    stores = [
+        pltpu.make_async_copy(a, b, out_sem.at[n])
+        for n, (a, b) in enumerate((
+            (gv_ref, gv_hbm), (gk_ref, gk_hbm), (gq_ref, gq_hbm), (gs_ref, gs_hbm), (smo_ref, smo_hbm), (gw_ref, gw_hbm),
+        ))
+    ]
+    stores[0].start()
     dst = jnp.where(causal, acc[...], 0.0).astype(BF16)
     gk_ref[...] = nn(dst, q_ref[...]) + kacc[...].T
     gq_ref[...] = (nn(k_ref[...].T, dst) + qacc[...]).T
@@ -481,6 +486,7 @@
     r = rrow[...] + urow[...]
     da = nn(frow[...] - r, upto, HIGHEST) + tail
     gs_ref[...] = r / dt - rate * da
+    start(stores[1:4])
     g_decay = jnp.sum(-rate * dt * da, axis=1, keepdims=True)
     g_skip = jnp.sum(xrow[...], axis=1, keepdims=True)
     lane = lax.broadcasted_iota(jnp.int32, (HEADS, 128), 1)
@@ -502,13 +508,15 @@
         last.extend(start([reach("y", d, rows[p].at[y], rows[p].at[y], 6 + p) for d in range(1, 4)]))
     small = small_start("z", s_z, small_sum(small, s_y), 11)
     smo_ref[...] = small_sum(small, s_z)
-    store.wait()
+    stores[4].start()
     wait(last)
     for n in range(4):
         gw_ref[16 * n : 16 * n + 8, :768] = w0[n]
         gw_ref[16 * n : 16 * n + 8, 768:] = w1[n, :, :256]
         gw_ref[16 * n + 8 : 16 * n + 16, :384] = w1[n, :, 256:]
         gw_ref[16 * n + 8 : 16 * n + 16, 384:] = w2[n]
+    stores[5].start()
+    wait(stores)
 
 
 def output_kernel(
@@ -562,7 +570,7 @@
             sds((HEADS, 128)), sds((64, MODEL)),
         ),
         in_specs=[anywhere] * 8,
-        out_specs=(anywhere,) + (inside,) * 5,
+        out_specs=(anywhere,) * 6,
         scratch_shapes=[
             vm((SPAN, INNER), BF16), vm((SPAN, STATE), BF16), vm((SPAN, STATE), BF16), row,
             vm((1, HEADS), F32), vm((1, HEADS), F32), vm((INNER, MODEL), BF16), vm((SPAN, MODEL), BF16),
@@ -574,6 +582,7 @@
             vm((SPAN, SPAN), F32), vm((SPAN, SPAN), F32), vm((STATE, SPAN), F32), vm((STATE, SPAN), F32),
             vm((CHIPS, 2, WIDTH, SPAN), F32), vm((CHIPS, WIDTH, SPAN), F32),
             vm((INNER, SPAN), F32), vm((SPAN, INNER), F32),
+            vm((SPAN, STATE), F32), vm((SPAN, STATE), F32), row, vm((HEADS, 128), F32), vm((64, MODEL), F32),
             vm((SPAN, MODEL), F32), vm((SPAN, MODEL), F32), vm((SPAN, STATE), F32), vm((SPAN, STATE), F32),
             row, vm((2 * SPAN, MODEL), BF16), *[vm((4, 4, 4, 8, w), F32) for w in wides],
             *[vm((4, 4, 8, w), F32) for w in wides],
@@ -585,7 +594,7 @@
             vm((2, 2, 4, 8, wides[0]), F32), vm((4, 2, 2, 8, wides[1]), F32), vm((4, 2, 2, 8, wides[2]), F32),
             vm((2, HEADS, 128), F32),
             *[vm((4, HEADS, 128), F32)] * 3,
-            dma((8,)), dma, dma((10,)), dma((10,)), dma((4, CHIPS)), dma((4, CHIPS)),
+            dma((8,)), dma((6,)), dma((10,)), dma((10,)), dma((4, CHIPS)), dma((4, CHIPS)),
             dma((54,)), dma((54,)), dma((12, 3)), dma((12, 3)),
         ],
         compiler_params=pltpu.CompilerParams(

time: 76.2 us -> 76.2 us (level)
  no operation moved by 1% of the time
where the time goes in v7:
time: 76.2 us; the launch traced here: 76 us
  Pallas kernels  75.4 us (99%)
    pallas_call x1, Pallas kernels, local(): pl.pallas_call(mixer_kernel, out_shape=(sds((SPAN, INNER)), sds((SPAN, ST...  72.7 us
    pallas_call x1, Pallas kernels, local(): pl.pallas_call(output_kernel, out_shape=(sds((SPAN, INNER)), sds((SPAN, S...  2.68 us

profile of v7, /device:TPU:0, one launch (start us, length us, event | category | flops | bytes accessed | tf_op | source)
XLA Modules:
  0.0 76.0 jit_solution(10887768859038248422)
XLA Ops:
  0.6 72.7 %mixer.1 = (f32[256,2048]{1,0:T(8,128)}, f32[256,128]{1,0:T(8,128)}, f32[256,128]{1,0:T(8,128)}, f32[32,256]{1,0:T(8,128)}, f32[32,128]{1,0:T(8,128)}, /*index=5*/f32[64,1024]{1,0:T(8,128)}) custom-call(bf16[256,2048]{1,0:T(8,128)(2,1)} %bitcast.13, bf16[256,128]{1,0:T(8,128)(2,1)} %bitcast.15, bf16[256,128]{1,0:T(8,128)(2,1)} %bitcast.16, ...), custom_call_target="tpu_custom_call" | custom-call | tf_op jit(solution)/shard_map/mixer/pallas_call | solution.py:566
  73.3 2.7 %output.1 = (f32[256,2048]{1,0:T(8,128)}, f32[256,128]{1,0:T(8,128)}, f32[256,128]{1,0:T(8,128)}, f32[32,256]{1,0:T(8,128)}, f32[1,32]{1,0:T(1,128)}, /*index=5*/f32[1,32]{1,0:T(1,128)}, f32[64,1024]{1,0:T(8,128)}) custom-call(f32[256,2048]{1,0:T(8,128)} %get-tuple-element.20.gv, f32[256,128]{1,0:T(8,128)} %get-tuple-element.21.gk, ...), custom_call_target="tpu_custom_call" | custom-call | tf_op jit(solution)/shard_map/output/pallas_call | solution.py:605
